TPU v7x, 32 devices: a whole 2x2x4 slice. The times are simulated.
32 devices in a mesh: gx: 4 (over z), gy: 8 (over y, x, core).
Axes of the slice: x: 2, y: 2, z: 4, core: 2. Of those that a mesh axis runs over, the one named last changes fastest.
Arguments:
- speed_factor: float32 [64, 128, 256], P('gx', 'gy'), may hold values from 0.05 to 0.17
- wave_before: float32 [64, 128, 256], P('gx', 'gy'), may hold values from -6 to 6
- wave_now: float32 [64, 128, 256], P('gx', 'gy'), may hold values from -6 to 6
- source_accel: float32 [2, 64, 128, 256], P(None, 'gx', 'gy'), may hold values from -4 to 4
- prior_image: float32 [64, 128, 256], P('gx', 'gy'), may hold values from -40 to 40
- conv_first: bfloat16 [27, 1, 8], replicated, may hold values from -1.25 to 1.25
- bias_first: float32 [8], replicated, may hold values from -3 to 3
- conv_middle: bfloat16 [27, 8, 8], replicated, may hold values from -0.4375 to 0.4375
- bias_middle: float32 [8], replicated, may hold values from -3 to 3
- conv_last: bfloat16 [27, 8, 1], replicated, may hold values from -0.4375 to 0.4375
Outputs:
- wave_next: float32 [64, 128, 256], P('gx', 'gy')
- wave_after: float32 [64, 128, 256], P('gx', 'gy')
- gradient: float32 [64, 128, 256], P('gx', 'gy')
- model_step: float32 [64, 128, 256], P('gx', 'gy')
All inputs are finite; a program needn't handle non-finite values.
Results may differ from a plain program's by a relative error of at most 0.0059.
Values may be sent and summed in bfloat16 or wider, within the bound.
A program may use at most 192 MiB of HBM per device.

v0:
```python
import functools

import jax
import jax.numpy as jnp
from jax import lax
from jax.experimental import pallas as pl
from jax.experimental.pallas import tpu as pltpu
from jax.sharding import PartitionSpec as P

COEFS = (-205.0 / 72.0, 8.0 / 5.0, -1.0 / 5.0, 8.0 / 315.0, -1.0 / 560.0)
MESH = pl.DeviceIdType.MESH
F32 = jnp.float32
BF16 = jnp.bfloat16
UNROLL = True
WAVE_UNROLL = 8


def shift_z(v, k):
    depth = v.shape[-1]
    lane = lax.broadcasted_iota(jnp.int32, v.shape, v.ndim - 1)
    rolled = pltpu.roll(v, (-k) % depth, v.ndim - 1)
    return jnp.where((lane + k >= 0) & (lane + k < depth), rolled, 0.0)


def laplace_z(center):
    total = 3.0 * COEFS[0] * center
    for k in range(1, 5):
        total = total + COEFS[k] * (shift_z(center, k) + shift_z(center, -k))
    return total


def laplace_xy(ext, x, ny):
    total = None
    for k in range(1, 5):
        cycle = ext[x + 4 + k, 8 : 8 + ny, :] + ext[x + 4 - k, 8 : 8 + ny, :]
        cycle = cycle + ext[x + 4, 8 + k : 8 + k + ny, :]
        cycle = cycle + ext[x + 4, 8 - k : 8 - k + ny, :]
        total = COEFS[k] * cycle if total is None else total + COEFS[k] * cycle
    return total


def kernel(
    n_gx,
    n_gy,
    speed_hbm,
    before_hbm,
    now_hbm,
    src_hbm,
    prior_hbm,
    raw,
    raw_b1,
    raw_b2,
    out_next,
    out_after,
    out_grad,
    out_step,
    speed,
    before,
    src,
    prior,
    load_sem,
    ext_a,
    ext_b,
    pack_a,
    pack_b,
    recv_a,
    recv_b,
    grad,
    pack_g,
    recv_g,
    h1,
    h2,
    w1,
    w2,
    w3,
    part,
    red_y,
    red_x,
    send_sem,
    recv_sem,
    ry_send,
    ry_recv,
    rx_send,
    rx_recv,
):
    nx, ny, depth = now_hbm.shape
    gx, gy = lax.axis_index("gx"), lax.axis_index("gy")
    barrier = pltpu.get_barrier_semaphore()
    own = pl.ds(8, ny)
    loads = [
        pltpu.make_async_copy(source, target, load_sem.at[i])
        for i, (source, target) in enumerate(
            (
                (now_hbm, ext_a.at[pl.ds(4, nx), own, :]),
                (before_hbm, before),
                (speed_hbm, speed),
                (src_hbm, src),
                (prior_hbm, prior),
            )
        )
    ]
    for load in loads:
        load.start()

    def there(dx, dy):
        ok = None
        for pos, d, n in ((gx, dx, n_gx), (gy, dy, n_gy)):
            if d:
                one = (pos + d >= 0) & (pos + d < n)
                ok = one if ok is None else ok & one
        return ok

    for i in range(1, n_gy):
        pl.semaphore_signal(
            barrier, inc=1, device_id=(gx, lax.rem(gy + i, n_gy)), device_id_type=MESH
        )
    for i in range(1, n_gx):
        pl.semaphore_signal(
            barrier, inc=1, device_id=(lax.rem(gx + i, n_gx), gy), device_id_type=MESH
        )
    diagonals = ((-1, -1), (-1, 1), (1, -1), (1, 1))
    for dx, dy in diagonals:

        @pl.when(there(dx, dy))
        def _(dx=dx, dy=dy):
            pl.semaphore_signal(barrier, inc=1, device_id=(gx + dx, gy + dy), device_id_type=MESH)

    class Copy:
        def __init__(self, ident, source, target, dx, dy):
            self.make = lambda: pltpu.make_async_remote_copy(
                src_ref=source,
                dst_ref=target,
                send_sem=send_sem.at[ident],
                recv_sem=recv_sem.at[ident],
                device_id=(gx + dx, gy + dy),
                device_id_type=MESH,
            )
            self.to = there(dx, dy)
            self.origin = there(-dx, -dy)
            self.target = target

        def start(self):
            @pl.when(self.to)
            def _():
                self.make().start()

        def clear(self):
            @pl.when(jnp.logical_not(self.origin))
            def _():
                self.target[...] = jnp.zeros(self.target.shape, self.target.dtype)

        def arrive(self):
            @pl.when(self.origin)
            def _():
                self.make().wait_recv()

        def sent(self):
            @pl.when(self.to)
            def _():
                self.make().wait_send()

    def wave_copies(base, ext, pack, recv):
        return (
            Copy(base, ext.at[pl.ds(nx, 4), own, :], ext.at[pl.ds(0, 4), own, :], 1, 0),
            Copy(base + 1, ext.at[pl.ds(4, 4), own, :], ext.at[pl.ds(nx + 4, 4), own, :], -1, 0),
            Copy(base + 2, pack.at[1], recv.at[0], 0, 1),
            Copy(base + 3, pack.at[0], recv.at[1], 0, -1),
        )

    copies_a = wave_copies(0, ext_a, pack_a, recv_a)
    copies_b = wave_copies(4, ext_b, pack_b, recv_b)
    row16 = pl.ds(0, ny)
    groups = nx // 4
    mid = pl.ds(1, groups)
    copies_g = (
        Copy(8, grad.at[pl.ds(nx, 4), row16, :], grad.at[pl.ds(0, 4), row16, :], 1, 0),
        Copy(9, grad.at[pl.ds(4, 4), row16, :], grad.at[pl.ds(nx + 4, 4), row16, :], -1, 0),
        Copy(10, pack_g.at[1], recv_g.at[0, mid], 0, 1),
        Copy(11, pack_g.at[0], recv_g.at[1, mid], 0, -1),
        Copy(12, pack_g.at[1, groups - 1], recv_g.at[0, 0], 1, 1),
        Copy(13, pack_g.at[1, 0], recv_g.at[0, groups + 1], -1, 1),
        Copy(14, pack_g.at[0, groups - 1], recv_g.at[1, 0], 1, -1),
        Copy(15, pack_g.at[0, 0], recv_g.at[1, groups + 1], -1, -1),
    )

    def pack_wave(ext, pack):
        half = nx // 2
        for i in range(half):
            for side, at in ((0, 8), (1, 8 + ny - 4)):
                pack[side, i] = jnp.concatenate(
                    [ext[4 + i, at : at + 4, :], ext[4 + half + i, at : at + 4, :]], axis=0
                )

    def unpack_wave(ext, recv):
        half = nx // 2
        for i in range(half):
            for side, at in ((0, 4), (1, 8 + ny)):
                tile = recv[side, i]
                ext[4 + i, at : at + 4, :] = tile[0:4]
                ext[4 + half + i, at : at + 4, :] = tile[4:8]

    loads[0].wait()
    pack_wave(ext_a, pack_a)
    for group in (copies_a, copies_b, copies_g):
        for c in group:
            c.clear()

    wanted = (n_gy - 1) + (n_gx - 1)
    for dx, dy in diagonals:
        wanted = wanted + there(dx, dy).astype(jnp.int32)
    pl.semaphore_wait(barrier, wanted)
    for c in copies_a:
        c.start()

    def band(out, slabs, e, rows, per_row, first_out, width, place):
        shape = (rows * per_row, 3 * width)
        col = lax.broadcasted_iota(jnp.int32, shape, 1)
        row = lax.broadcasted_iota(jnp.int32, shape, 0)
        slot = col - jnp.where(col >= width, width, 0) - jnp.where(col >= 2 * width, width, 0)
        y_out = (row >> 3 if per_row == 8 else row) + first_out
        gap = place(slot) - y_out
        total = jnp.zeros(shape, F32)
        for b in range(3):
            slab = slabs[3 * b + e]
            if per_row == 8:
                full = jnp.concatenate([slab] * rows, axis=0)
            else:
                full = jnp.broadcast_to(slab, shape)
            total = jnp.where(gap == b - 1, full, total)
        out[e * shape[0] : (e + 1) * shape[0], :] = total.astype(BF16)

    def grad_slot(slot):
        return jnp.where(
            slot < ny, slot, jnp.where(slot < ny + 4, slot - ny - 4, jnp.where(slot < ny + 8, slot - 4, 999))
        )

    r1, r2 = ny + 4, ny + 2
    m1, m2 = 8 * r1, 8 * r2
    def third(index, size):
        return jnp.where(index >= size, 1, 0) + jnp.where(index >= 2 * size, 1, 0)

    def iota(shape, dim):
        return lax.broadcasted_iota(jnp.int32, shape, dim)

    def turned(rows):
        eye = jnp.where(iota((8, 8), 0) == iota((8, 8), 1), 1.0, 0.0).astype(BF16)
        return lax.dot_general(
            eye, rows.astype(BF16), (((1,), (1,)), ((), ())), preferred_element_type=F32
        )

    def stacked(flat, step):
        tall = jnp.concatenate([flat] * 9, axis=0)
        tap = iota(tall.shape, 1) >> step
        return jnp.where(tap - 9 * third(tap, 9) == iota(tall.shape, 0) >> 3, tall, 0.0).astype(BF16)

    def matches(count, step, width):
        shape = (count, 3 * width)
        tap, col = iota(shape, 0), iota(shape, 1)
        hit = third(tap >> step, 9) == third(col, width)
        return hit & ((tap & 7) == (col & 7)) if step else hit

    def one_hot(hit):
        return jnp.where(hit, 1.0, 0.0).astype(BF16)

    def column(bias):
        wide = jnp.broadcast_to(bias[...], (8, 8))
        return jnp.sum(jnp.where(iota((8, 8), 0) == iota((8, 8), 1), wide, 0.0), axis=1, keepdims=True)

    b1, b2 = column(raw_b1), column(raw_b2)
    rows = jnp.concatenate([raw[k].astype(F32) for k in range(27)], axis=0)
    wide2 = jnp.dot(
        stacked(turned(rows[:, 0:8]), 3), one_hot(matches(216, 3, m1)), preferred_element_type=F32
    )
    tap = iota((16, 216), 1) >> 3
    own_tap = one_hot(tap - 9 * third(tap, 9) == iota((16, 216), 0))
    wide3 = jnp.dot(
        own_tap,
        jnp.where(matches(216, 3, m2), rows[:, 8:9], 0.0).astype(BF16),
        preferred_element_type=F32,
    )
    tap = iota((72, 216), 1) >> 3
    own_row = (tap - 9 * third(tap, 9)) * 8 + (iota((72, 216), 1) & 7) == iota((72, 216), 0)
    same_a = third(iota((216, 6 * ny), 0) >> 3, 9) == third(iota((216, 6 * ny), 1), 2 * ny)
    wide1 = jnp.dot(
        one_hot(own_row),
        jnp.where(same_a, rows[:, 9:10], 0.0).astype(BF16),
        preferred_element_type=F32,
    )
    s1 = [wide1[8 * k : 8 * k + 8] for k in range(9)]
    s2 = [wide2[8 * k : 8 * k + 8] for k in range(9)]
    s3 = [wide3[k : k + 1] for k in range(9)]
    for e in range(3):
        band(w1, s1, e, r1, 8, -2, 2 * ny, grad_slot)
        band(w2, s2, e, r2, 8, -1, r1 * 8, lambda s: (s >> 3) - 2)
        band(w3, s3, e, ny, 1, 0, r2 * 8, lambda s: (s >> 3) - 1)

    for load in loads[1:]:
        load.wait()

    def inner_one(x, carry):
        center = ext_a[x + 4, 8 : 8 + ny, :]
        out_next[x] = 2.0 * center - before[x] + speed[x] * laplace_z(center)
        return carry

    lax.fori_loop(0, nx, inner_one, 0, unroll=WAVE_UNROLL)
    for c in copies_a:
        c.arrive()
    unpack_wave(ext_a, recv_a)

    def step_one(x, carry):
        value = out_next[x] + speed[x] * laplace_xy(ext_a, x, ny)
        out_next[x] = value
        ext_b[x + 4, 8 : 8 + ny, :] = value
        return carry

    lax.fori_loop(0, nx, step_one, 0, unroll=WAVE_UNROLL)
    for c in copies_b[:2]:
        c.start()
    pack_wave(ext_b, pack_b)
    for c in copies_b[2:]:
        c.start()

    def inner_two(x, carry):
        center = out_next[x]
        out_after[x] = 2.0 * center - ext_a[x + 4, 8 : 8 + ny, :] + speed[x] * laplace_z(center)
        return carry

    lax.fori_loop(0, nx, inner_two, 0, unroll=WAVE_UNROLL)
    for c in copies_b:
        c.arrive()
    unpack_wave(ext_b, recv_b)

    def step_two(x, carry):
        center = out_next[x]
        value = out_after[x] + speed[x] * laplace_xy(ext_b, x, ny)
        out_after[x] = value
        gradient = prior[x] + src[0, x] * center + src[1, x] * value
        out_grad[x] = gradient
        grad[x + 4, 0:ny, :] = gradient.astype(BF16)
        return carry

    lax.fori_loop(0, nx, step_two, 0, unroll=WAVE_UNROLL)
    for c in copies_g[:2]:
        c.start()
    for t in range(groups):
        for side, at in ((0, 0), (1, ny - 4)):
            pack_g[side, t] = jnp.concatenate(
                [out_grad[4 * t + j, at : at + 4, :] for j in range(4)], axis=0
            ).astype(BF16)
    for c in copies_g[2:]:
        c.start()
    for c in copies_g:
        c.arrive()
    for t in range(groups + 2):
        low = recv_g[0, t].astype(F32)
        high = recv_g[1, t].astype(F32)
        for j in range(4):
            grad[4 * t + j, ny : 2 * ny, :] = jnp.concatenate(
                [low[4 * j : 4 * j + 4], high[4 * j : 4 * j + 4], jnp.zeros((ny - 8, depth), F32)],
                axis=0,
            ).astype(BF16)

    x_min = jnp.where(gx == 0, 0, -8)
    x_max = jnp.where(gx == n_gx - 1, nx, nx + 8)
    y_min = jnp.where(gy == 0, 0, -8)
    y_max = jnp.where(gy == n_gy - 1, ny, ny + 8)

    def conv_plane(weight, rhs, rows):
        res = jnp.dot(weight[...], rhs, preferred_element_type=F32)
        return (
            res[rows : 2 * rows] + shift_z(res[:rows], -1) + shift_z(res[2 * rows :], 1)
        )

    def hidden(value, bias, rows, first, x):
        y = (lax.broadcasted_iota(jnp.int32, value.shape, 0) >> 3) + first
        inside = (y >= y_min) & (y < y_max) & (x >= x_min) & (x < x_max)
        full = jnp.concatenate([jnp.broadcast_to(bias, (8, depth))] * rows, axis=0)
        return jnp.where(inside, jnp.maximum(value + full, 0.0), 0.0).astype(BF16)

    def layer_one(p, carry):
        rhs = grad[pl.ds(p + 1, 3)].reshape(6 * ny, depth)
        h1[p] = hidden(conv_plane(w1, rhs, m1), b1, r1, -2, p - 2)
        return carry

    lax.fori_loop(0, nx + 4, layer_one, 0, unroll=UNROLL)

    def layer_two(p, carry):
        rhs = h1[pl.ds(p, 3)].reshape(3 * m1, depth)
        h2[p] = hidden(conv_plane(w2, rhs, m2), b2, r2, -1, p - 1)
        return carry

    lax.fori_loop(0, nx + 2, layer_two, 0, unroll=UNROLL)

    zero = jnp.zeros((ny, depth), F32)

    def layer_three(p, carry):
        gg, gd, dd = carry
        rhs = h2[pl.ds(p, 3)].reshape(3 * m2, depth)
        g = out_grad[p]
        d = conv_plane(w3, rhs, ny) + g
        out_step[p] = d
        return gg + g * g, gd + g * d, dd + d * d

    sums = lax.fori_loop(0, nx, layer_three, (zero, zero, zero), unroll=UNROLL)
    row = lax.broadcasted_iota(jnp.int32, (8, depth), 0)
    tile = jnp.zeros((8, depth), F32)
    for i, s in enumerate(sums):
        tile = jnp.where(row == i, jnp.sum(s, axis=0, keepdims=True), tile)
    folded = tile[:, 0:128]
    for i in range(1, depth // 128):
        folded = folded + tile[:, 128 * i : 128 * i + 128]

    def reduce_over(value, slot, slots, me, n, sends, recvs, peer_id):
        part[slot] = value
        slots[me] = value
        todo = []
        for i in range(1, n):
            c = pltpu.make_async_remote_copy(
                src_ref=part.at[slot],
                dst_ref=slots.at[me],
                send_sem=sends.at[i],
                recv_sem=recvs.at[i],
                device_id=peer_id(lax.rem(me + i, n)),
                device_id_type=MESH,
            )
            c.start()
            todo.append(c)
        for i, c in enumerate(todo):
            back = pltpu.make_async_remote_copy(
                src_ref=part.at[slot],
                dst_ref=slots.at[lax.rem(me + n - (i + 1), n)],
                send_sem=sends.at[i + 1],
                recv_sem=recvs.at[i + 1],
                device_id=peer_id(lax.rem(me + i + 1, n)),
                device_id_type=MESH,
            )
            back.wait_recv()
        total = slots[0]
        for i in range(1, n):
            total = total + slots[i]
        return total, todo

    over_y, todo_y = reduce_over(folded, 0, red_y, gy, n_gy, ry_send, ry_recv, lambda j: (gx, j))
    total, todo_x = reduce_over(over_y, 1, red_x, gx, n_gx, rx_send, rx_recv, lambda j: (j, gy))
    sums = jnp.sum(total, axis=1, keepdims=True)
    damping = 8.0 * float(nx * n_gx * ny * n_gy * depth)
    scale = sums[1:2] / (sums[0:1] + sums[2:3] + damping)

    def finish(p, carry):
        out_step[p] = scale * out_step[p]
        return carry

    lax.fori_loop(0, nx, finish, 0, unroll=4)
    for group in (copies_a, copies_b, copies_g):
        for c in group:
            c.sent()
    for c in todo_y + todo_x:
        c.wait_send()


def hand_on(*refs):
    for source, target in zip(refs[:4], refs[4:]):
        target[...] = source[...]


def shards(n_gx, n_gy, speed, before, now, src, prior, w_first, b_first, w_mid, b_mid, w_last):
    nx, ny, depth = now.shape
    out = jax.ShapeDtypeStruct(now.shape, F32)
    vmem = pl.BlockSpec(memory_space=pltpu.VMEM)
    half, groups = nx // 2, nx // 4
    r1, r2 = ny + 4, ny + 2
    ch = b_first.shape[0]
    outs = pl.pallas_call(
        functools.partial(kernel, n_gx, n_gy),
        out_shape=(out,) * 4,
        in_specs=[pl.BlockSpec(memory_space=pl.ANY)] * 5 + [vmem] * 3,
        out_specs=(vmem,) * 4,
        scratch_shapes=[
            pltpu.VMEM(now.shape, F32),
            pltpu.VMEM(now.shape, F32),
            pltpu.VMEM(src.shape, F32),
            pltpu.VMEM(now.shape, F32),
            pltpu.SemaphoreType.DMA((5,)),
            pltpu.VMEM((nx + 8, ny + 16, depth), F32),
            pltpu.VMEM((nx + 8, ny + 16, depth), F32),
            pltpu.VMEM((2, half, 8, depth), F32),
            pltpu.VMEM((2, half, 8, depth), F32),
            pltpu.VMEM((2, half, 8, depth), F32),
            pltpu.VMEM((2, half, 8, depth), F32),
            pltpu.VMEM((nx + 8, 2 * ny, depth), BF16),
            pltpu.VMEM((2, groups, 16, depth), BF16),
            pltpu.VMEM((2, groups + 2, 16, depth), BF16),
            pltpu.VMEM((nx + 4, r1 * ch, depth), BF16),
            pltpu.VMEM((nx + 2, r2 * ch, depth), BF16),
            pltpu.VMEM((3 * r1 * ch, 6 * ny), BF16),
            pltpu.VMEM((3 * r2 * ch, 3 * r1 * ch), BF16),
            pltpu.VMEM((3 * ny, 3 * r2 * ch), BF16),
            pltpu.VMEM((2, 8, 128), F32),
            pltpu.VMEM((n_gy, 8, 128), F32),
            pltpu.VMEM((n_gx, 8, 128), F32),
            pltpu.SemaphoreType.DMA((16,)),
            pltpu.SemaphoreType.DMA((16,)),
            pltpu.SemaphoreType.DMA((n_gy,)),
            pltpu.SemaphoreType.DMA((n_gy,)),
            pltpu.SemaphoreType.DMA((n_gx,)),
            pltpu.SemaphoreType.DMA((n_gx,)),
        ],
        compiler_params=pltpu.CompilerParams(
            collective_id=0, has_side_effects=True, vmem_limit_bytes=60 * 1024 * 1024
        ),
    )(
        speed,
        before,
        now,
        src,
        prior,
        jnp.concatenate([w_mid, w_last, w_first.reshape(27, ch, 1)], axis=2),
        b_first.reshape(1, ch),
        b_mid.reshape(1, ch),
    )
    block = pl.BlockSpec((nx // 4, ny, depth), lambda i: (i, 0, 0))
    return pl.pallas_call(
        hand_on,
        grid=(4,),
        out_shape=(out,) * 4,
        in_specs=[block] * 4,
        out_specs=(block,) * 4,
    )(*outs)


def solution(mesh):
    brick = P("gx", "gy", None)
    return jax.shard_map(
        functools.partial(shards, mesh.shape["gx"], mesh.shape["gy"]),
        mesh=mesh,
        in_specs=(brick, brick, brick, P(None, "gx", "gy", None), brick, P(), P(), P(), P(), P()),
        out_specs=(brick,) * 4,
        check_vma=False,
    )
```

profile of v0, /device:TPU:0, one launch (start us, length us, event | category | flops | bytes accessed | tf_op | source)
XLA Modules:
  0.0 36.9 jit_solution(17061647696929609338)
XLA Ops:
  0.6 0.0 copy-start.1
  0.6 0.7 %copy-done.1 = bf16[27,1,8]{0,2,1:T(8,128)(2,1)S(1)} copy-done((bf16[27,1,8]{0,2,1:T(8,128)(2,1)S(1)}, bf16[27,1,8]{0,2,1:T(8,128)(2,1)}, u32[]{:S(2)}) %copy-start.1) | copy-done | bytes 456
  1.3 0.0 copy-start
  1.3 0.2 copy.24
  1.5 0.6 %copy-done = bf16[27,8,8]{0,2,1:T(8,128)(2,1)S(1)} copy-done((bf16[27,8,8]{0,2,1:T(8,128)(2,1)S(1)}, bf16[27,8,8]{0,2,1:T(8,128)(2,1)}, u32[]{:S(2)}) %copy-start) | copy-done | bytes 3480
  2.0 0.0 copy-start.2
  2.0 0.1 copy.22
  2.2 0.5 %copy-done.2 = bf16[27,8,1]{0,1,2:T(8,128)(2,1)S(1)} copy-done((bf16[27,8,1]{0,1,2:T(8,128)(2,1)S(1)}, bf16[27,8,1]{0,1,2:T(8,128)(2,1)}, u32[]{:S(2)}) %copy-start.2) | copy-done | bytes 456
  2.7 0.2 copy.23
  2.9 0.7 %pad_maximum_fusion.raw = bf16[27,8,10]{2,1,0:T(8,128)(2,1)} fusion(bf16[27,8,1]{2,1,0:T(8,128)(2,1)S(1)} %copy.24, bf16[27,8,1]{2,1,0:T(8,128)(2,1)S(1)} %copy.23, bf16[27,8,8]{2,1,0:T(8,128)(2,1)S(1)} %copy.22), kind=kLoop, calls=%fused_computation | loop fusion | flops 12960 | bytes 8640 | tf_op jit(solution)/shard_map/concatenate | solution.py:517
  3.6 29.9 %shard_map.129 = (f32[16,16,256]{2,1,0:T(8,128)}, f32[16,16,256]{2,1,0:T(8,128)}, f32[16,16,256]{2,1,0:T(8,128)}, f32[16,16,256]{2,1,0:T(8,128)}) custom-call(f32[16,16,256]{2,1,0:T(8,128)} %speed_hbm.1, f32[16,16,256]{2,1,0:T(8,128)} %before_hbm.1, f32[16,16,256]{2,1,0:T(8,128)} %now_hbm.1, f32[2,16,16,256]{3,2,1,0:T(8,128)} %src_hbm.1, ...), custom_call_target="tpu_custom_call" | custom-call | tf_op jit(solution)/shard_map/pallas_call | solution.py:473
  33.6 3.3 %shard_map.130 = (f32[16,16,256]{2,1,0:T(8,128)}, f32[16,16,256]{2,1,0:T(8,128)}, f32[16,16,256]{2,1,0:T(8,128)}, f32[16,16,256]{2,1,0:T(8,128)}) custom-call(f32[16,16,256]{2,1,0:T(8,128)} %get-tuple-element.8.refs_0_, f32[16,16,256]{2,1,0:T(8,128)} %get-tuple-element.9.refs_1_, f32[16,16,256]{2,1,0:T(8,128)} %get-tuple-element.10.refs_2_, ...), custom_call_target="tpu_custom_call" | custom-call | tf_op jit(solution)/shard_map/pallas_call | solution.py:522
Async XLA Ops:
  0.6 0.7 %copy-start.1 = (bf16[27,1,8]{0,2,1:T(8,128)(2,1)S(1)}, bf16[27,1,8]{0,2,1:T(8,128)(2,1)}, u32[]{:S(2)}) copy-start(bf16[27,1,8]{0,2,1:T(8,128)(2,1)} %param.15) | copy-start | bytes 1300
  1.3 0.7 %copy-start = (bf16[27,8,8]{0,2,1:T(8,128)(2,1)S(1)}, bf16[27,8,8]{0,2,1:T(8,128)(2,1)}, u32[]{:S(2)}) copy-start(bf16[27,8,8]{0,2,1:T(8,128)(2,1)} %param.17) | copy-start | bytes 10372
  2.0 0.7 %copy-start.2 = (bf16[27,8,1]{0,1,2:T(8,128)(2,1)S(1)}, bf16[27,8,1]{0,1,2:T(8,128)(2,1)}, u32[]{:S(2)}) copy-start(bf16[27,8,1]{0,1,2:T(8,128)(2,1)} %param.19) | copy-start | bytes 1300
where the time goes:
time: 37.4 us; the launch traced here: 36.9 us
  Pallas kernels  33.3 us (89%)
  local copies, waits for them, and re-layouts  2.23 us (6%)
  other arithmetic  0.73 us (2%)
  between operations  0.65 us (2%)
    pallas_call x1, Pallas kernels, shards(): pl.pallas_call(functools.partial(kernel, n_gx, n_gy), out_shape=(out,) *...  29.9 us
    pallas_call x1, Pallas kernels, shards(): pl.pallas_call(hand_on, grid=(4,), out_shape=(out,) * 4, in_specs=[block]...  3.34 us
    unnamed x8, local copies, waits for them, and re-layouts  2.07 us

commit v1 on v0

v1 whole, which is shorter than its diff:
```python
import functools

import jax
import jax.numpy as jnp
from jax import lax
from jax.experimental import pallas as pl
from jax.experimental.pallas import tpu as pltpu
from jax.sharding import PartitionSpec as P

COEFS = (-205.0 / 72.0, 8.0 / 5.0, -1.0 / 5.0, 8.0 / 315.0, -1.0 / 560.0)
MESH = pl.DeviceIdType.MESH
F32 = jnp.float32
BF16 = jnp.bfloat16
UNROLL = True
WAVE_UNROLL = 8


def shift_z(v, k):
    depth = v.shape[-1]
    lane = lax.broadcasted_iota(jnp.int32, v.shape, v.ndim - 1)
    rolled = pltpu.roll(v, (-k) % depth, v.ndim - 1)
    return jnp.where((lane + k >= 0) & (lane + k < depth), rolled, 0.0)


def iota(shape, dim):
    return lax.broadcasted_iota(jnp.int32, shape, dim)


def one_hot(hit):
    return jnp.where(hit, 1.0, 0.0).astype(BF16)


def third(index, size):
    return jnp.where(index >= size, 1, 0) + jnp.where(index >= 2 * size, 1, 0)


def laplace_z(center):
    total = 3.0 * COEFS[0] * center
    for k in range(1, 5):
        total = total + COEFS[k] * (shift_z(center, k) + shift_z(center, -k))
    return total


def laplace_xy(ext, x, ny):
    total = None
    for k in range(1, 5):
        cycle = ext[x + 4 + k, 8 : 8 + ny, :] + ext[x + 4 - k, 8 : 8 + ny, :]
        cycle = cycle + ext[x + 4, 8 + k : 8 + k + ny, :]
        cycle = cycle + ext[x + 4, 8 - k : 8 - k + ny, :]
        total = COEFS[k] * cycle if total is None else total + COEFS[k] * cycle
    return total


def kernel(
    n_gx,
    n_gy,
    speed_hbm,
    before_hbm,
    now_hbm,
    src_hbm,
    prior_hbm,
    first_hbm,
    mid_hbm,
    last_hbm,
    bias1_hbm,
    bias2_hbm,
    out_next,
    out_after,
    out_grad,
    out_dir,
    out_sums,
    speed,
    before,
    src,
    prior,
    raw1,
    raw2,
    raw3,
    bias1,
    bias2,
    load_sem,
    ext_a,
    ext_b,
    pack_a,
    pack_b,
    recv_a,
    recv_b,
    grad,
    pack_g,
    recv_gx,
    recv_g,
    h1,
    h2,
    w1,
    w2,
    w3,
    part,
    red,
    send_sem,
    recv_sem,
    red_send,
    red_recv,
):
    nx, ny, depth = now_hbm.shape
    gx, gy = lax.axis_index("gx"), lax.axis_index("gy")
    barrier = pltpu.get_barrier_semaphore()
    own = pl.ds(8, ny)
    loads = [
        pltpu.make_async_copy(source, target, load_sem.at[i])
        for i, (source, target) in enumerate(
            (
                (now_hbm, ext_a.at[pl.ds(4, nx), own, :]),
                (before_hbm, before),
                (speed_hbm, speed),
                (src_hbm, src),
                (prior_hbm, prior),
                (first_hbm, raw1),
                (mid_hbm, raw2),
                (last_hbm, raw3),
                (bias1_hbm, bias1),
                (bias2_hbm, bias2),
            )
        )
    ]
    for load in loads:
        load.start()

    def there(dx, dy):
        ok = None
        for pos, d, n in ((gx, dx, n_gx), (gy, dy, n_gy)):
            if d:
                one = (pos + d >= 0) & (pos + d < n)
                ok = one if ok is None else ok & one
        return ok

    count = n_gx * n_gy
    me = gx * n_gy + gy

    def peer(i):
        flat = lax.rem(me + i, count)
        return (lax.div(flat, n_gy), lax.rem(flat, n_gy))

    for i in range(1, count):
        pl.semaphore_signal(barrier, inc=1, device_id=peer(i), device_id_type=MESH)

    class Copy:
        def __init__(self, ident, source, target, dx, dy):
            self.make = lambda: pltpu.make_async_remote_copy(
                src_ref=source,
                dst_ref=target,
                send_sem=send_sem.at[ident],
                recv_sem=recv_sem.at[ident],
                device_id=(gx + dx, gy + dy),
                device_id_type=MESH,
            )
            self.to = there(dx, dy)
            self.origin = there(-dx, -dy)
            self.target = target

        def start(self):
            @pl.when(self.to)
            def _():
                self.make().start()

        def clear(self):
            @pl.when(jnp.logical_not(self.origin))
            def _():
                self.target[...] = jnp.zeros(self.target.shape, self.target.dtype)

        def arrive(self):
            @pl.when(self.origin)
            def _():
                self.make().wait_recv()

        def sent(self):
            @pl.when(self.to)
            def _():
                self.make().wait_send()

    def wave_copies(base, ext, pack, recv):
        return (
            Copy(base, ext.at[pl.ds(nx, 4), own, :], ext.at[pl.ds(0, 4), own, :], 1, 0),
            Copy(base + 1, ext.at[pl.ds(4, 4), own, :], ext.at[pl.ds(nx + 4, 4), own, :], -1, 0),
            Copy(base + 2, pack.at[1], recv.at[0], 0, 1),
            Copy(base + 3, pack.at[0], recv.at[1], 0, -1),
        )

    copies_a = wave_copies(0, ext_a, pack_a, recv_a)
    copies_b = wave_copies(4, ext_b, pack_b, recv_b)
    groups = nx // 4
    mid = pl.ds(1, groups)
    same_z = pl.ds(ny, ny)
    copies_g = (
        Copy(12, pack_g.at[1, groups - 1], recv_g.at[0, 0], 1, 1),
        Copy(13, pack_g.at[1, 0], recv_g.at[0, groups + 1], -1, 1),
        Copy(14, pack_g.at[0, groups - 1], recv_g.at[1, 0], 1, -1),
        Copy(15, pack_g.at[0, 0], recv_g.at[1, groups + 1], -1, -1),
        Copy(10, pack_g.at[1], recv_g.at[0, mid], 0, 1),
        Copy(11, pack_g.at[0], recv_g.at[1, mid], 0, -1),
        Copy(8, grad.at[pl.ds(nx, 3), same_z, :], recv_gx.at[0], 1, 0),
        Copy(9, grad.at[pl.ds(3, 3), same_z, :], recv_gx.at[1], -1, 0),
    )

    def pack_wave(ext, pack):
        half = nx // 2
        for i in range(half):
            for side, at in ((0, 8), (1, 8 + ny - 4)):
                pack[side, i] = jnp.concatenate(
                    [ext[4 + i, at : at + 4, :], ext[4 + half + i, at : at + 4, :]], axis=0
                )

    def unpack_wave(ext, recv):
        half = nx // 2
        for i in range(half):
            for side, at in ((0, 4), (1, 8 + ny)):
                tile = recv[side, i]
                ext[4 + i, at : at + 4, :] = tile[0:4]
                ext[4 + half + i, at : at + 4, :] = tile[4:8]

    loads[0].wait()
    pack_wave(ext_a, pack_a)
    for group in (copies_a, copies_b, copies_g):
        for c in group:
            c.clear()

    pl.semaphore_wait(barrier, count - 1)
    for c in copies_a:
        c.start()

    for load in loads[1:]:
        load.wait()

    r1, r2 = ny + 4, ny + 2
    m1, m2 = 8 * r1, 8 * r2
    slots = 3 * ny + 32
    blk = 6

    def column(bias):
        wide = jnp.broadcast_to(bias[...], (8, 8))
        return jnp.sum(jnp.where(iota((8, 8), 0) == iota((8, 8), 1), wide, 0.0), axis=1, keepdims=True)

    b1, b2 = column(bias1), column(bias2)

    def place_first(shape, dim):
        col = iota(shape, dim)
        a = third(col, slots)
        slot = col - slots * a
        side = slot - 3 * ny
        q = side & 7
        e = jnp.where(slot < 3 * ny, third(slot, ny), side >> 3)
        y = jnp.where(slot < 3 * ny, slot - ny * e, jnp.where(q < 4, q - 4, q + ny - 4))
        y = jnp.where(side >= 24, 999, y)
        return a, e, y, col

    a_in, e_in, _, _ = place_first((27, 3 * slots), 0 + 1)
    taps = [
        jnp.dot(
            raw1[...],
            one_hot(iota((27, 3 * slots), 0) == 9 * a_in + 3 * b + e_in),
            preferred_element_type=F32,
        )
        for b in range(3)
    ]
    _, _, y_in, col = place_first((8, 3 * slots), 1)
    top = b1.astype(BF16).astype(F32)
    rest = b1 - top
    middle = rest.astype(BF16).astype(F32)
    base = slots + 3 * ny + 24
    biases = jnp.where(col == base, top, jnp.where(col == base + 1, middle, jnp.where(col == base + 2, rest - middle, 0.0)))

    def rows_first(y):
        total = biases
        for b in range(3):
            total = jnp.where(y_in - y == b - 1, taps[b], total)
        return total

    for y in range(0, r1, 2):
        w1[8 * y : 8 * y + 16, :] = jnp.concatenate(
            [rows_first(y - 2), rows_first(y - 1)], axis=0
        ).astype(BF16)

    k2 = 8 * (blk + 2)
    same_c = (iota((64, 3 * k2), 0) >> 3) == (iota((64, 3 * k2), 1) & 7)
    a_in = third(iota((27, 3 * k2), 1), k2)
    col = iota((8, 3 * k2), 1)
    y_in = (col - k2 * third(col, k2)) >> 3
    table = []
    for t in range(9):
        full = jnp.dot(
            raw2[...], one_hot(iota((27, 3 * k2), 0) == 9 * a_in + t), preferred_element_type=F32
        )
        full = jnp.where(same_c, full, 0.0)
        total = full[0:8]
        for c in range(1, 8):
            total = total + full[8 * c : 8 * c + 8]
        table.append(total)

    def rows_mid(i):
        e, y = i // blk, i % blk
        total = jnp.zeros((8, 3 * k2), F32)
        for b in range(3):
            total = jnp.where(y_in - y == b, table[3 * b + e], total)
        return total

    for i in range(0, 3 * blk, 2):
        w2[8 * i : 8 * i + 16, :] = jnp.concatenate([rows_mid(i), rows_mid(i + 1)], axis=0).astype(BF16)

    same_c = iota((8, 3 * m2), 0) == (iota((8, 3 * m2), 1) & 7)
    a_in = third(iota((27, 3 * m2), 1), m2)
    col = iota((ny, 3 * m2), 1)
    gap = ((col - m2 * third(col, m2)) >> 3) - iota((ny, 3 * m2), 0)
    for e in range(3):
        total = jnp.zeros((ny, 3 * m2), F32)
        for b in range(3):
            full = jnp.dot(
                raw3[...],
                one_hot(iota((27, 3 * m2), 0) == 9 * a_in + 3 * b + e),
                preferred_element_type=F32,
            )
            line = jnp.sum(jnp.where(same_c, full, 0.0), axis=0, keepdims=True)
            total = jnp.where(gap == b, jnp.broadcast_to(line, total.shape), total)
        w3[ny * e : ny * e + ny, :] = total.astype(BF16)

    def inner_one(x, carry):
        center = ext_a[x + 4, 8 : 8 + ny, :]
        out_next[x] = 2.0 * center - before[x] + speed[x] * laplace_z(center)
        return carry

    lax.fori_loop(0, nx, inner_one, 0, unroll=WAVE_UNROLL)
    for c in copies_a:
        c.arrive()
    unpack_wave(ext_a, recv_a)

    def step_one(x, carry):
        value = out_next[x] + speed[x] * laplace_xy(ext_a, x, ny)
        out_next[x] = value
        ext_b[x + 4, 8 : 8 + ny, :] = value
        return carry

    lax.fori_loop(0, nx, step_one, 0, unroll=WAVE_UNROLL)
    for c in copies_b[:2]:
        c.start()
    pack_wave(ext_b, pack_b)
    for c in copies_b[2:]:
        c.start()

    def inner_two(x, carry):
        center = out_next[x]
        out_after[x] = 2.0 * center - ext_a[x + 4, 8 : 8 + ny, :] + speed[x] * laplace_z(center)
        return carry

    lax.fori_loop(0, nx, inner_two, 0, unroll=WAVE_UNROLL)
    for c in copies_b:
        c.arrive()
    unpack_wave(ext_b, recv_b)

    def store_own(plane, value):
        for e in range(3):
            rows = value if e == 1 else shift_z(value, e - 1)
            grad[plane, ny * e : ny * e + ny, :] = rows.astype(BF16)

    def step_two(x, carry):
        center = out_next[x]
        value = out_after[x] + speed[x] * laplace_xy(ext_b, x, ny)
        out_after[x] = value
        gradient = prior[x] + src[0, x] * center + src[1, x] * value
        out_grad[x] = gradient
        store_own(x + 3, gradient)
        return carry

    lax.fori_loop(0, nx, step_two, 0, unroll=WAVE_UNROLL)
    for t in range(groups):
        for side, at in ((0, 0), (1, ny - 4)):
            pack_g[side, t] = jnp.concatenate(
                [out_grad[4 * t + j, at : at + 4, :] for j in range(4)], axis=0
            ).astype(BF16)
    for c in copies_g:
        c.start()
    for c in copies_g:
        c.arrive()
    ones = jnp.where(iota((8, depth), 0) < 3, 1.0, 0.0)
    for plane in range(nx + 6):
        t, j = (plane + 1) // 4, (plane + 1) % 4
        low = recv_g[0, t].astype(F32)[4 * j : 4 * j + 4]
        high = recv_g[1, t].astype(F32)[4 * j : 4 * j + 4]
        side = jnp.concatenate([low, high], axis=0)
        grad[plane, 3 * ny : 3 * ny + 32, :] = jnp.concatenate(
            [shift_z(side, -1), side, shift_z(side, 1), ones], axis=0
        ).astype(BF16)
    for i in range(3):
        store_own(i, recv_gx[0, i].astype(F32))
        store_own(nx + 3 + i, recv_gx[1, i].astype(F32))

    big = 3.0e38
    x_low = jnp.where(gx == 0, 0.0, big)
    x_high = jnp.where(gx == n_gx - 1, 0.0, big)
    y_low = jnp.where(gy == 0, 0.0, big)
    y_high = jnp.where(gy == n_gy - 1, 0.0, big)

    def conv_plane(weight, rhs, rows):
        res = jnp.dot(weight[...], rhs, preferred_element_type=F32)
        return (
            res[rows : 2 * rows] + shift_z(res[:rows], -1) + shift_z(res[2 * rows :], 1)
        )

    def limit(value, cap):
        return value if cap is None else jnp.minimum(value, cap)

    for p in range(nx + 4):
        res = jnp.maximum(
            jnp.dot(w1[...], grad[p : p + 3].reshape(3 * slots, depth), preferred_element_type=F32), 0.0
        )
        cap = x_low if p < 2 else x_high if p >= nx + 2 else None
        res = limit(res, cap)
        h1[p, 0:16] = jnp.minimum(res[0:16], y_low).astype(BF16)
        h1[p, 16 : m1 - 16] = res[16 : m1 - 16].astype(BF16)
        h1[p, m1 - 16 : m1] = jnp.minimum(res[m1 - 16 : m1], y_high).astype(BF16)

    full2 = jnp.concatenate([jnp.broadcast_to(b2, (8, depth))] * blk, axis=0)
    for p in range(nx + 2):
        cap = x_low if p < 1 else x_high if p >= nx + 1 else None
        for y in range(0, r2, blk):
            rhs = h1[p : p + 3, 8 * y : 8 * y + k2, :].reshape(3 * k2, depth)
            res = limit(jnp.maximum(conv_plane(w2, rhs, 8 * blk) + full2, 0.0), cap)
            if y == 0:
                res = jnp.concatenate([jnp.minimum(res[0:8], y_low), res[8:]], axis=0)
            if y + blk == r2:
                res = jnp.concatenate([res[: 8 * blk - 8], jnp.minimum(res[8 * blk - 8 :], y_high)], axis=0)
            h2[p, 8 * y : 8 * y + 8 * blk] = res.astype(BF16)

    zero = jnp.zeros((ny, depth), F32)

    def layer_three(p, carry):
        gg, gd, dd = carry
        rhs = h2[pl.ds(p, 3)].reshape(3 * m2, depth)
        g = out_grad[p]
        d = conv_plane(w3, rhs, ny) + g
        out_dir[p] = d
        return gg + g * g, gd + g * d, dd + d * d

    sums = lax.fori_loop(0, nx, layer_three, (zero, zero, zero), unroll=UNROLL)
    row, lane = iota((8, 128), 0), iota((8, 128), 1)
    tile = jnp.zeros((8, 128), F32)
    for i, s in enumerate(sums):
        line = jnp.sum(s, axis=0, keepdims=True)
        folded = line[:, 0:128]
        for j in range(1, depth // 128):
            folded = folded + line[:, 128 * j : 128 * j + 128]
        tile = jnp.where(row == i, folded, tile)
    wide = jnp.broadcast_to(jnp.sum(tile, axis=1, keepdims=True), (8, 128))
    mine = jnp.sum(jnp.where(row == lane, wide, 0.0), axis=0, keepdims=True)
    part[...] = mine
    for i in range(1, count):
        pltpu.make_async_remote_copy(
            src_ref=part,
            dst_ref=red.at[i - 1],
            send_sem=red_send.at[i - 1],
            recv_sem=red_recv.at[i - 1],
            device_id=peer(i),
            device_id_type=MESH,
        ).start()
    waits = [
        pltpu.make_async_remote_copy(
            src_ref=part,
            dst_ref=red.at[i - 1],
            send_sem=red_send.at[i - 1],
            recv_sem=red_recv.at[i - 1],
            device_id=peer(i),
            device_id_type=MESH,
        )
        for i in range(1, count)
    ]
    for c in waits:
        c.wait_recv()
    total = mine
    for i in range(count - 1):
        total = total + red[i]
    spread = jnp.where(row == lane, jnp.broadcast_to(total, (8, 128)), 0.0)
    out_sums[...] = jnp.broadcast_to(jnp.sum(spread, axis=1, keepdims=True), (8, 128))
    for group in (copies_a, copies_b, copies_g):
        for c in group:
            c.sent()
    for c in waits:
        c.wait_send()


def hand_on(damping, sums, v_next, v_after, v_grad, v_dir, o_next, o_after, o_grad, o_step, scaled, sem):
    moves = [
        pltpu.make_async_copy(source, target, sem.at[i])
        for i, (source, target) in enumerate(((v_next, o_next), (v_after, o_after), (v_grad, o_grad)))
    ]
    for move in moves:
        move.start()
    scale = sums[1:2, 0:1] / (sums[0:1, 0:1] + sums[2:3, 0:1] + damping)
    nx = v_dir.shape[0]
    step = nx // 4
    for i in range(4):
        at = pl.ds(i * step, step)
        scaled[at] = scale.reshape(1, 1, 1) * v_dir[at]
        move = pltpu.make_async_copy(scaled.at[at], o_step.at[at], sem.at[3 + i])
        move.start()
        moves.append(move)
    for move in moves:
        move.wait()


def shards(n_gx, n_gy, speed, before, now, src, prior, w_first, b_first, w_mid, b_mid, w_last):
    nx, ny, depth = now.shape
    out = jax.ShapeDtypeStruct(now.shape, F32)
    vmem = pl.BlockSpec(memory_space=pltpu.VMEM)
    hbm = pl.BlockSpec(memory_space=pltpu.HBM)
    half, groups = nx // 2, nx // 4
    r1, r2 = ny + 4, ny + 2
    ch = b_first.shape[0]
    slots, blk = 3 * ny + 32, 6
    count = n_gx * n_gy
    held = pltpu.VMEM(now.shape, F32)
    *outs, sums = pl.pallas_call(
        functools.partial(kernel, n_gx, n_gy),
        out_shape=(held,) * 4 + (pltpu.VMEM((8, 128), F32),),
        in_specs=[hbm] * 10,
        out_specs=(vmem,) * 5,
        scratch_shapes=[
            pltpu.VMEM(now.shape, F32),
            pltpu.VMEM(now.shape, F32),
            pltpu.VMEM(src.shape, F32),
            pltpu.VMEM(now.shape, F32),
            pltpu.VMEM((ch, 27), BF16),
            pltpu.VMEM((ch * ch, 27), BF16),
            pltpu.VMEM((ch, 27), BF16),
            pltpu.VMEM((1, ch), F32),
            pltpu.VMEM((1, ch), F32),
            pltpu.SemaphoreType.DMA((10,)),
            pltpu.VMEM((nx + 8, ny + 16, depth), F32),
            pltpu.VMEM((nx + 8, ny + 16, depth), F32),
            pltpu.VMEM((2, half, 8, depth), F32),
            pltpu.VMEM((2, half, 8, depth), F32),
            pltpu.VMEM((2, half, 8, depth), F32),
            pltpu.VMEM((2, half, 8, depth), F32),
            pltpu.VMEM((nx + 6, slots, depth), BF16),
            pltpu.VMEM((2, groups, 16, depth), BF16),
            pltpu.VMEM((2, 3, ny, depth), BF16),
            pltpu.VMEM((2, groups + 2, 16, depth), BF16),
            pltpu.VMEM((nx + 4, r1 * ch, depth), BF16),
            pltpu.VMEM((nx + 2, r2 * ch, depth), BF16),
            pltpu.VMEM((r1 * ch, 3 * slots), BF16),
            pltpu.VMEM((3 * blk * ch, 3 * (blk + 2) * ch), BF16),
            pltpu.VMEM((3 * ny, 3 * r2 * ch), BF16),
            pltpu.VMEM((1, 128), F32),
            pltpu.VMEM((count - 1, 1, 128), F32),
            pltpu.SemaphoreType.DMA((16,)),
            pltpu.SemaphoreType.DMA((16,)),
            pltpu.SemaphoreType.DMA((count - 1,)),
            pltpu.SemaphoreType.DMA((count - 1,)),
        ],
        compiler_params=pltpu.CompilerParams(
            collective_id=0, has_side_effects=True, vmem_limit_bytes=40 * 1024 * 1024
        ),
    )(
        *(
            pltpu.with_memory_space_constraint(v, pltpu.HBM)
            for v in (
                speed,
                before,
                now,
                src,
                prior,
                w_first.transpose(1, 2, 0).reshape(ch, 27),
                w_mid.transpose(1, 2, 0).reshape(ch * ch, 27),
                w_last.transpose(2, 1, 0).reshape(ch, 27),
                b_first.reshape(1, ch),
                b_mid.reshape(1, ch),
            )
        )
    )
    return pl.pallas_call(
        functools.partial(hand_on, 8.0 * float(nx * n_gx * ny * n_gy * depth)),
        out_shape=(out,) * 4,
        in_specs=[vmem] * 5,
        out_specs=(hbm,) * 4,
        scratch_shapes=[pltpu.VMEM(now.shape, F32), pltpu.SemaphoreType.DMA((7,))],
    )(*(pltpu.with_memory_space_constraint(v, pltpu.VMEM) for v in (sums, *outs)))


def solution(mesh):
    brick = P("gx", "gy", None)
    return jax.shard_map(
        functools.partial(shards, mesh.shape["gx"], mesh.shape["gy"]),
        mesh=mesh,
        in_specs=(brick, brick, brick, P(None, "gx", "gy", None), brick, P(), P(), P(), P(), P()),
        out_specs=(brick,) * 4,
        check_vma=False,
    )
```

time: 37.4 us -> 26.7 us (0.71)
  Pallas kernels: 33.3 us -> 25.9 us
  local copies, waits for them, and re-layouts: 2.23 us -> 0 us
  other arithmetic: 0.73 us -> 0 us
    pallas_call x2, Pallas kernels: 33.3 us -> 25.9 us  [the longest x1 24.9 us: shards(): pl.pallas_call(functools.partial(kernel, n_gx, n_gy), out_shape=(held,) *...]
    unnamed x8 -> x0, local copies, waits for them, and re-layouts: 2.07 us -> none
    concatenate x1 -> x0, other arithmetic: 0.73 us -> none  [shards(): jnp.concatenate([w_mid, w_last, w_first.reshape(27, ch, 1)], axis=2)]
where the time goes in v1:
time: 26.7 us; the launch traced here: 26.6 us
  Pallas kernels  25.9 us (97%)
  between operations  0.64 us (2%)
    pallas_call x1, Pallas kernels, shards(): pl.pallas_call(functools.partial(kernel, n_gx, n_gy), out_shape=(held,) *...  24.9 us
    pallas_call x1, Pallas kernels, shards(): pl.pallas_call(functools.partial(hand_on, 8.0 * float(nx * n_gx * ny * n_...  1.02 us

profile of v1, /device:TPU:0, one launch (start us, length us, event | category | flops | bytes accessed | tf_op | source)
XLA Modules:
  0.0 26.6 jit_solution(16982275685378283914)
XLA Ops:
  0.6 24.9 %shard_map.129 = (f32[16,16,256]{2,1,0:T(8,128)S(1)}, f32[16,16,256]{2,1,0:T(8,128)S(1)}, f32[16,16,256]{2,1,0:T(8,128)S(1)}, f32[16,16,256]{2,1,0:T(8,128)S(1)}, f32[8,128]{1,0:T(8,128)S(1)}) custom-call(f32[16,16,256]{2,1,0:T(8,128)} %speed_hbm.1, f32[16,16,256]{2,1,0:T(8,128)} %before_hbm.1, f32[16,16,256]{2,1,0:T(8,128)} %now_hbm.1, ...), custom_call_target="tpu_custom_call" | custom-call | tf_op jit(solution)/shard_map/pallas_call | solution.py:518
  25.5 1.0 %shard_map.130 = (f32[16,16,256]{2,1,0:T(8,128)}, f32[16,16,256]{2,1,0:T(8,128)}, f32[16,16,256]{2,1,0:T(8,128)}, f32[16,16,256]{2,1,0:T(8,128)}) custom-call(f32[8,128]{1,0:T(8,128)S(1)} %get-tuple-element.9.sums, f32[16,16,256]{2,1,0:T(8,128)S(1)} %get-tuple-element.10.v_next, f32[16,16,256]{2,1,0:T(8,128)S(1)} %get-tuple-element.11.v_after, ...), custom_call_target="tpu_custom_call" | custom-call | tf_op jit(solution)/shard_map/pallas_call | solution.py:576

commit v2 on v1

--- a/solution.py
+++ b/solution.py
@@ -81,10 +81,13 @@
     load_sem,
     ext_a,
     ext_b,
-    pack_a,
-    pack_b,
-    recv_a,
-    recv_b,
+    pack_x,
+    pack_y,
+    recv_x,
+    recv_y,
+    recv_c,
+    from_own_x,
+    from_own_y,
     grad,
     pack_g,
     recv_gx,
@@ -104,21 +107,21 @@
     nx, ny, depth = now_hbm.shape
     gx, gy = lax.axis_index("gx"), lax.axis_index("gy")
     barrier = pltpu.get_barrier_semaphore()
-    own = pl.ds(8, ny)
+    brick = pl.ds(8, ny)
     loads = [
         pltpu.make_async_copy(source, target, load_sem.at[i])
         for i, (source, target) in enumerate(
             (
-                (now_hbm, ext_a.at[pl.ds(4, nx), own, :]),
+                (now_hbm, ext_a.at[pl.ds(4, nx), brick, :]),
                 (before_hbm, before),
                 (speed_hbm, speed),
-                (src_hbm, src),
-                (prior_hbm, prior),
                 (first_hbm, raw1),
                 (mid_hbm, raw2),
                 (last_hbm, raw3),
                 (bias1_hbm, bias1),
                 (bias2_hbm, bias2),
+                (src_hbm, src),
+                (prior_hbm, prior),
             )
         )
     ]
@@ -177,19 +180,19 @@
             def _():
                 self.make().wait_send()
 
-    def wave_copies(base, ext, pack, recv):
-        return (
-            Copy(base, ext.at[pl.ds(nx, 4), own, :], ext.at[pl.ds(0, 4), own, :], 1, 0),
-            Copy(base + 1, ext.at[pl.ds(4, 4), own, :], ext.at[pl.ds(nx + 4, 4), own, :], -1, 0),
-            Copy(base + 2, pack.at[1], recv.at[0], 0, 1),
-            Copy(base + 3, pack.at[0], recv.at[1], 0, -1),
-        )
-
-    copies_a = wave_copies(0, ext_a, pack_a, recv_a)
-    copies_b = wave_copies(4, ext_b, pack_b, recv_b)
     groups = nx // 4
     mid = pl.ds(1, groups)
     same_z = pl.ds(ny, ny)
+    copies_w = (
+        Copy(0, pack_y.at[1, groups - 1, 0], recv_c.at[0, 0], 1, 1),
+        Copy(1, pack_y.at[1, 0, 0], recv_c.at[1, 0], -1, 1),
+        Copy(2, pack_y.at[0, groups - 1, 0], recv_c.at[0, 1], 1, -1),
+        Copy(3, pack_y.at[0, 0, 0], recv_c.at[1, 1], -1, -1),
+        Copy(4, pack_y.at[1], recv_y.at[0], 0, 1),
+        Copy(5, pack_y.at[0], recv_y.at[1], 0, -1),
+        Copy(6, pack_x.at[1], recv_x.at[0], 1, 0),
+        Copy(7, pack_x.at[0], recv_x.at[1], -1, 0),
+    )
     copies_g = (
         Copy(12, pack_g.at[1, groups - 1], recv_g.at[0, 0], 1, 1),
         Copy(13, pack_g.at[1, 0], recv_g.at[0, groups + 1], -1, 1),
@@ -201,33 +204,76 @@
         Copy(9, grad.at[pl.ds(3, 3), same_z, :], recv_gx.at[1], -1, 0),
     )
 
-    def pack_wave(ext, pack):
-        half = nx // 2
-        for i in range(half):
-            for side, at in ((0, 8), (1, 8 + ny - 4)):
-                pack[side, i] = jnp.concatenate(
-                    [ext[4 + i, at : at + 4, :], ext[4 + half + i, at : at + 4, :]], axis=0
-                )
-
-    def unpack_wave(ext, recv):
-        half = nx // 2
-        for i in range(half):
-            for side, at in ((0, 4), (1, 8 + ny)):
-                tile = recv[side, i]
-                ext[4 + i, at : at + 4, :] = tile[0:4]
-                ext[4 + half + i, at : at + 4, :] = tile[4:8]
-
-    loads[0].wait()
-    pack_wave(ext_a, pack_a)
-    for group in (copies_a, copies_b, copies_g):
+    row8 = iota((8, depth), 0)
+
+    def half_turn(v):
+        return pltpu.roll(v, 4, 0)
+
+    def edge(v):
+        return jnp.where(row8 < 4, v[0:8], v[ny - 8 : ny])
+
+    def pack_four(e):
+        low = [jnp.where(row8 < 4, e[i], half_turn(e[i + 1])) for i in (0, 2)]
+        high = [jnp.where(row8 < 4, half_turn(e[i]), e[i + 1]) for i in (0, 2)]
+        return [jnp.concatenate(v, axis=0).astype(BF16) for v in (low, high)]
+
+    def unpack_four(low, high):
+        sides = []
+        for i in (0, 8):
+            a, b = low.astype(F32)[i : i + 8], high.astype(F32)[i : i + 8]
+            sides.append(jnp.where(row8 < 4, b, half_turn(a)))
+            sides.append(jnp.where(row8 < 4, half_turn(b), a))
+        return sides
+
+    def across(v):
+        total = jnp.zeros((8, depth), F32)
+        for k in range(1, 5):
+            down, up = pltpu.roll(v, k, 0), pltpu.roll(v, 8 - k, 0)
+            total = total + COEFS[k] * jnp.where(row8 < k, down, jnp.where(row8 >= 8 - k, up, 0.0))
+        return total
+
+    def spread(e):
+        parts = [jnp.where(row8 < 4, e, 0.0), jnp.where(row8 < 4, 0.0, e)]
+        if ny > 16:
+            parts.insert(1, jnp.zeros((ny - 16, depth), F32))
+        return jnp.concatenate(parts, axis=0)
+
+    blank = jnp.zeros((ny + 16, depth), F32)
+    for i in range(4):
+        ext_a[i] = blank
+        ext_a[nx + 4 + i] = blank
+    for x in range(nx):
+        ext_a[x + 4, 0:8] = blank[0:8]
+        ext_a[x + 4, ny + 8 : ny + 16] = blank[0:8]
+    for load in loads[:3]:
+        load.wait()
+
+    for t in range(groups):
+        edges = [[], [], []]
+        for x in range(4 * t, 4 * t + 4):
+            center = ext_a[x + 4, 8 : 8 + ny, :]
+            factor = speed[x]
+            partial = (
+                2.0 * center - before[x] + factor * (laplace_z(center) + laplace_xy(ext_a, x, ny))
+            )
+            out_next[x] = partial
+            for i, v in enumerate((center, partial, factor)):
+                edges[i].append(edge(v))
+                if x < 4:
+                    pack_x[0, x, i] = v.astype(BF16)
+                if x >= nx - 4:
+                    pack_x[1, x - nx + 4, i] = v.astype(BF16)
+        for i in range(3):
+            pack_y[0, t, i], pack_y[1, t, i] = pack_four(edges[i])
+
+    for group in (copies_w, copies_g):
         for c in group:
             c.clear()
-
     pl.semaphore_wait(barrier, count - 1)
-    for c in copies_a:
+    for c in copies_w:
         c.start()
 
-    for load in loads[1:]:
+    for load in loads[3:8]:
         load.wait()
 
     r1, r2 = ny + 4, ny + 2
@@ -248,7 +294,7 @@
         side = slot - 3 * ny
         q = side & 7
         e = jnp.where(slot < 3 * ny, third(slot, ny), side >> 3)
-        y = jnp.where(slot < 3 * ny, slot - ny * e, jnp.where(q < 4, q - 4, q + ny - 4))
+        y = jnp.where(slot < 3 * ny, slot - ny * e, jnp.where(q < 4, q + ny, q - 8))
         y = jnp.where(side >= 24, 999, y)
         return a, e, y, col
 
@@ -321,38 +367,48 @@
             total = jnp.where(gap == b, jnp.broadcast_to(line, total.shape), total)
         w3[ny * e : ny * e + ny, :] = total.astype(BF16)
 
-    def inner_one(x, carry):
-        center = ext_a[x + 4, 8 : 8 + ny, :]
-        out_next[x] = 2.0 * center - before[x] + speed[x] * laplace_z(center)
-        return carry
-
-    lax.fori_loop(0, nx, inner_one, 0, unroll=WAVE_UNROLL)
-    for c in copies_a:
+    own = slice(8, 8 + ny)
+    outside = [x for x in range(-4, nx + 4) if x < 0 or x >= nx]
+
+    def reach(x, inside):
+        return [(k, x + d * k) for k in range(1, 5) for d in (-1, 1) if inside(x + d * k)]
+
+    for i, x in enumerate(outside):
+        total = jnp.zeros((ny, depth), F32)
+        for k, at in reach(x, lambda v: 0 <= v < nx):
+            total = total + COEFS[k] * ext_a[at + 4, own]
+        from_own_x[i] = total
+    for x in range(nx):
+        from_own_y[x] = across(edge(ext_a[x + 4, own]))
+    for load in loads[8:]:
+        load.wait()
+
+    for c in copies_w:
         c.arrive()
-    unpack_wave(ext_a, recv_a)
-
-    def step_one(x, carry):
-        value = out_next[x] + speed[x] * laplace_xy(ext_a, x, ny)
-        out_next[x] = value
-        ext_b[x + 4, 8 : 8 + ny, :] = value
-        return carry
-
-    lax.fori_loop(0, nx, step_one, 0, unroll=WAVE_UNROLL)
-    for c in copies_b[:2]:
-        c.start()
-    pack_wave(ext_b, pack_b)
-    for c in copies_b[2:]:
-        c.start()
-
-    def inner_two(x, carry):
-        center = out_next[x]
-        out_after[x] = 2.0 * center - ext_a[x + 4, 8 : 8 + ny, :] + speed[x] * laplace_z(center)
-        return carry
-
-    lax.fori_loop(0, nx, inner_two, 0, unroll=WAVE_UNROLL)
-    for c in copies_b:
-        c.arrive()
-    unpack_wave(ext_b, recv_b)
+    corner = {}
+    for i, first in enumerate((-4, nx)):
+        for j, v in enumerate(unpack_four(recv_c[i, 0], recv_c[i, 1])):
+            corner[first + j] = v
+    halo_x = {x: recv_x.at[i // 4, i % 4] for i, x in enumerate(outside)}
+    for i, x in enumerate(outside):
+        felt = from_own_x[i] + spread(across(corner[x]))
+        ext_b[x + 4, own] = halo_x[x][1].astype(F32) + halo_x[x][2].astype(F32) * felt
+    for t in range(groups):
+        sides = [unpack_four(recv_y[0, t, i], recv_y[1, t, i]) for i in range(3)]
+        for j in range(4):
+            x = 4 * t + j
+            felt = from_own_y[x]
+            for k, at in reach(x, lambda v: v in corner):
+                felt = felt + COEFS[k] * corner[at]
+            side = sides[1][j] + sides[2][j] * felt
+            ext_b[x + 4, 0:8] = side
+            ext_b[x + 4, ny + 8 : ny + 16] = side
+            felt = spread(across(sides[0][j]))
+            for k, at in reach(x, lambda v: v in corner):
+                felt = felt + COEFS[k] * halo_x[at][0].astype(F32)
+            value = out_next[x] + speed[x] * felt
+            out_next[x] = value
+            ext_b[x + 4, own] = value
 
     def store_own(plane, value):
         for e in range(3):
@@ -361,7 +417,7 @@
 
     def step_two(x, carry):
         center = out_next[x]
-        value = out_after[x] + speed[x] * laplace_xy(ext_b, x, ny)
+        value = 2.0 * center - ext_a[x + 4, own] + speed[x] * (laplace_z(center) + laplace_xy(ext_b, x, ny))
         out_after[x] = value
         gradient = prior[x] + src[0, x] * center + src[1, x] * value
         out_grad[x] = gradient
@@ -370,23 +426,19 @@
 
     lax.fori_loop(0, nx, step_two, 0, unroll=WAVE_UNROLL)
     for t in range(groups):
-        for side, at in ((0, 0), (1, ny - 4)):
-            pack_g[side, t] = jnp.concatenate(
-                [out_grad[4 * t + j, at : at + 4, :] for j in range(4)], axis=0
-            ).astype(BF16)
+        pack_g[0, t], pack_g[1, t] = pack_four([edge(out_grad[4 * t + j]) for j in range(4)])
     for c in copies_g:
         c.start()
     for c in copies_g:
         c.arrive()
     ones = jnp.where(iota((8, depth), 0) < 3, 1.0, 0.0)
-    for plane in range(nx + 6):
-        t, j = (plane + 1) // 4, (plane + 1) % 4
-        low = recv_g[0, t].astype(F32)[4 * j : 4 * j + 4]
-        high = recv_g[1, t].astype(F32)[4 * j : 4 * j + 4]
-        side = jnp.concatenate([low, high], axis=0)
-        grad[plane, 3 * ny : 3 * ny + 32, :] = jnp.concatenate(
-            [shift_z(side, -1), side, shift_z(side, 1), ones], axis=0
-        ).astype(BF16)
+    for t in range(groups + 2):
+        for j, side in enumerate(unpack_four(recv_g[0, t], recv_g[1, t])):
+            plane = 4 * t + j - 1
+            if 0 <= plane < nx + 6:
+                grad[plane, 3 * ny : 3 * ny + 32, :] = jnp.concatenate(
+                    [shift_z(side, -1), side, shift_z(side, 1), ones], axis=0
+                ).astype(BF16)
     for i in range(3):
         store_own(i, recv_gx[0, i].astype(F32))
         store_own(nx + 3 + i, recv_gx[1, i].astype(F32))
@@ -477,7 +529,7 @@
         total = total + red[i]
     spread = jnp.where(row == lane, jnp.broadcast_to(total, (8, 128)), 0.0)
     out_sums[...] = jnp.broadcast_to(jnp.sum(spread, axis=1, keepdims=True), (8, 128))
-    for group in (copies_a, copies_b, copies_g):
+    for group in (copies_w, copies_g):
         for c in group:
             c.sent()
     for c in waits:
@@ -509,7 +561,7 @@
     out = jax.ShapeDtypeStruct(now.shape, F32)
     vmem = pl.BlockSpec(memory_space=pltpu.VMEM)
     hbm = pl.BlockSpec(memory_space=pltpu.HBM)
-    half, groups = nx // 2, nx // 4
+    groups = nx // 4
     r1, r2 = ny + 4, ny + 2
     ch = b_first.shape[0]
     slots, blk = 3 * ny + 32, 6
@@ -533,10 +585,13 @@
             pltpu.SemaphoreType.DMA((10,)),
             pltpu.VMEM((nx + 8, ny + 16, depth), F32),
             pltpu.VMEM((nx + 8, ny + 16, depth), F32),
-            pltpu.VMEM((2, half, 8, depth), F32),
-            pltpu.VMEM((2, half, 8, depth), F32),
-            pltpu.VMEM((2, half, 8, depth), F32),
-            pltpu.VMEM((2, half, 8, depth), F32),
+            pltpu.VMEM((2, 4, 3, ny, depth), BF16),
+            pltpu.VMEM((2, groups, 3, 16, depth), BF16),
+            pltpu.VMEM((2, 4, 3, ny, depth), BF16),
+            pltpu.VMEM((2, groups, 3, 16, depth), BF16),
+            pltpu.VMEM((2, 2, 16, depth), BF16),
+            pltpu.VMEM((8, ny, depth), F32),
+            pltpu.VMEM((nx, 8, depth), F32),
             pltpu.VMEM((nx + 6, slots, depth), BF16),
             pltpu.VMEM((2, groups, 16, depth), BF16),
             pltpu.VMEM((2, 3, ny, depth), BF16),

time: 26.7 us -> 25.1 us (0.940)
  Pallas kernels: 25.9 us -> 24.3 us
    pallas_call x1, Pallas kernels: 24.9 us -> 23.3 us  [shards(): pl.pallas_call(functools.partial(kernel, n_gx, n_gy), out_shape=(held,) *...]
where the time goes in v2:
time: 25.1 us; the launch traced here: 25 us
  Pallas kernels  24.3 us (97%)
  between operations  0.64 us (3%)
    pallas_call x1, Pallas kernels, shards(): pl.pallas_call(functools.partial(kernel, n_gx, n_gy), out_shape=(held,) *...  23.3 us
    pallas_call x1, Pallas kernels, shards(): pl.pallas_call(functools.partial(hand_on, 8.0 * float(nx * n_gx * ny * n_...  1.02 us

profile of v2, /device:TPU:0, one launch (start us, length us, event | category | flops | bytes accessed | tf_op | source)
XLA Modules:
  0.0 25.0 jit_solution(11509872696286173119)
XLA Ops:
  0.6 23.3 %shard_map.129 = (f32[16,16,256]{2,1,0:T(8,128)S(1)}, f32[16,16,256]{2,1,0:T(8,128)S(1)}, f32[16,16,256]{2,1,0:T(8,128)S(1)}, f32[16,16,256]{2,1,0:T(8,128)S(1)}, f32[8,128]{1,0:T(8,128)S(1)}) custom-call(f32[16,16,256]{2,1,0:T(8,128)} %speed_hbm.1, f32[16,16,256]{2,1,0:T(8,128)} %before_hbm.1, f32[16,16,256]{2,1,0:T(8,128)} %now_hbm.1, ...), custom_call_target="tpu_custom_call" | custom-call | tf_op jit(solution)/shard_map/pallas_call | solution.py:570
  23.9 1.0 %shard_map.130 = (f32[16,16,256]{2,1,0:T(8,128)}, f32[16,16,256]{2,1,0:T(8,128)}, f32[16,16,256]{2,1,0:T(8,128)}, f32[16,16,256]{2,1,0:T(8,128)}) custom-call(f32[8,128]{1,0:T(8,128)S(1)} %get-tuple-element.9.sums, f32[16,16,256]{2,1,0:T(8,128)S(1)} %get-tuple-element.10.v_next, f32[16,16,256]{2,1,0:T(8,128)S(1)} %get-tuple-element.11.v_after, ...), custom_call_target="tpu_custom_call" | custom-call | tf_op jit(solution)/shard_map/pallas_call | solution.py:631

commit v3 on v2

--- a/solution.py
+++ b/solution.py
@@ -12,7 +12,8 @@
 F32 = jnp.float32
 BF16 = jnp.bfloat16
 UNROLL = True
-WAVE_UNROLL = 8
+WAVE_UNROLL = 4
+FAR = 3
 
 
 def shift_z(v, k):
@@ -32,13 +33,6 @@
 
 def third(index, size):
     return jnp.where(index >= size, 1, 0) + jnp.where(index >= 2 * size, 1, 0)
-
-
-def laplace_z(center):
-    total = 3.0 * COEFS[0] * center
-    for k in range(1, 5):
-        total = total + COEFS[k] * (shift_z(center, k) + shift_z(center, -k))
-    return total
 
 
 def laplace_xy(ext, x, ny):
@@ -88,6 +82,8 @@
     recv_c,
     from_own_x,
     from_own_y,
+    stencil,
+    lap_z,
     grad,
     pack_g,
     recv_gx,
@@ -143,8 +139,40 @@
         flat = lax.rem(me + i, count)
         return (lax.div(flat, n_gy), lax.rem(flat, n_gy))
 
-    for i in range(1, count):
-        pl.semaphore_signal(barrier, inc=1, device_id=peer(i), device_id_type=MESH)
+    def greet(x, y):
+        pl.semaphore_signal(barrier, inc=1, device_id=(x, y), device_id_type=MESH)
+
+    def within(pos, n, d):
+        return jnp.minimum(pos, d) + jnp.minimum(n - 1 - pos, d) + 1
+
+    for dx, dy in ((0, 1), (0, -1), (1, 0), (-1, 0), (1, 1), (1, -1), (-1, 1), (-1, -1)):
+
+        @pl.when(there(dx, dy))
+        def _(dx=dx, dy=dy):
+            greet(gx + dx, gy + dy)
+
+    def far(pos, j):
+        return (j - pos > FAR) | (pos - j > FAR)
+
+    for j in range(n_gy):
+
+        @pl.when(far(gy, j))
+        def _(j=j):
+            for i in range(n_gx):
+                greet(i, j)
+
+        if n_gx > FAR + 1:
+
+            @pl.when(jnp.logical_not(far(gy, j)))
+            def _(j=j):
+                for i in range(n_gx):
+
+                    @pl.when(far(gx, i))
+                    def _(i=i):
+                        greet(i, j)
+
+    wanted = within(gx, n_gx, 1) * within(gy, n_gy, 1) - 1
+    wanted = wanted + count - within(gx, n_gx, FAR) * within(gy, n_gy, FAR)
 
     class Copy:
         def __init__(self, ident, source, target, dx, dy):
@@ -238,6 +266,24 @@
             parts.insert(1, jnp.zeros((ny - 16, depth), F32))
         return jnp.concatenate(parts, axis=0)
 
+    gap = iota((depth, depth), 0) - iota((depth, depth), 1)
+    taps = jnp.zeros((depth, depth), F32)
+    for k in range(5):
+        taps = jnp.where((gap == k) | (gap == -k), COEFS[k] * (1.0 if k else 3.0), taps)
+    stencil[0] = taps.astype(BF16)
+    stencil[1] = (taps - taps.astype(BF16).astype(F32)).astype(BF16)
+
+    def along_z(field):
+        v = field.reshape(nx * ny, depth)
+        high = v.astype(BF16)
+        low = (v - high.astype(F32)).astype(BF16)
+
+        def times(x, i):
+            return jnp.dot(x, stencil[i], preferred_element_type=F32)
+
+        total = times(high, 0) + times(high, 1) + times(low, 0)
+        lap_z[...] = total.reshape(nx, ny, depth)
+
     blank = jnp.zeros((ny + 16, depth), F32)
     for i in range(4):
         ext_a[i] = blank
@@ -248,13 +294,14 @@
     for load in loads[:3]:
         load.wait()
 
+    along_z(ext_a[4 : 4 + nx, 8 : 8 + ny, :])
     for t in range(groups):
         edges = [[], [], []]
         for x in range(4 * t, 4 * t + 4):
             center = ext_a[x + 4, 8 : 8 + ny, :]
             factor = speed[x]
             partial = (
-                2.0 * center - before[x] + factor * (laplace_z(center) + laplace_xy(ext_a, x, ny))
+                2.0 * center - before[x] + factor * (lap_z[x] + laplace_xy(ext_a, x, ny))
             )
             out_next[x] = partial
             for i, v in enumerate((center, partial, factor)):
@@ -269,7 +316,7 @@
     for group in (copies_w, copies_g):
         for c in group:
             c.clear()
-    pl.semaphore_wait(barrier, count - 1)
+    pl.semaphore_wait(barrier, wanted)
     for c in copies_w:
         c.start()
 
@@ -415,9 +462,11 @@
             rows = value if e == 1 else shift_z(value, e - 1)
             grad[plane, ny * e : ny * e + ny, :] = rows.astype(BF16)
 
+    along_z(out_next[...])
+
     def step_two(x, carry):
         center = out_next[x]
-        value = 2.0 * center - ext_a[x + 4, own] + speed[x] * (laplace_z(center) + laplace_xy(ext_b, x, ny))
+        value = 2.0 * center - ext_a[x + 4, own] + speed[x] * (lap_z[x] + laplace_xy(ext_b, x, ny))
         out_after[x] = value
         gradient = prior[x] + src[0, x] * center + src[1, x] * value
         out_grad[x] = gradient
@@ -592,6 +641,8 @@
             pltpu.VMEM((2, 2, 16, depth), BF16),
             pltpu.VMEM((8, ny, depth), F32),
             pltpu.VMEM((nx, 8, depth), F32),
+            pltpu.VMEM((2, depth, depth), BF16),
+            pltpu.VMEM(now.shape, F32),
             pltpu.VMEM((nx + 6, slots, depth), BF16),
             pltpu.VMEM((2, groups, 16, depth), BF16),
             pltpu.VMEM((2, 3, ny, depth), BF16),

time: 25.1 us -> 24.2 us (0.964)
  Pallas kernels: 24.3 us -> 23.4 us
    pallas_call x1, Pallas kernels: 23.3 us -> 22.4 us  [shards(): pl.pallas_call(functools.partial(kernel, n_gx, n_gy), out_shape=(held,) *...]
where the time goes in v3:
time: 24.2 us; the launch traced here: 24.1 us
  Pallas kernels  23.4 us (97%)
  between operations  0.64 us (3%)
    pallas_call x1, Pallas kernels, shards(): pl.pallas_call(functools.partial(kernel, n_gx, n_gy), out_shape=(held,) *...  22.4 us
    pallas_call x1, Pallas kernels, shards(): pl.pallas_call(functools.partial(hand_on, 8.0 * float(nx * n_gx * ny * n_...  1.02 us

profile of v3, /device:TPU:0, one launch (start us, length us, event | category | flops | bytes accessed | tf_op | source)
XLA Modules:
  0.0 24.1 jit_solution(12120508164484904428)
XLA Ops:
  0.6 22.4 %shard_map.129 = (f32[16,16,256]{2,1,0:T(8,128)S(1)}, f32[16,16,256]{2,1,0:T(8,128)S(1)}, f32[16,16,256]{2,1,0:T(8,128)S(1)}, f32[16,16,256]{2,1,0:T(8,128)S(1)}, f32[8,128]{1,0:T(8,128)S(1)}) custom-call(f32[16,16,256]{2,1,0:T(8,128)} %speed_hbm.1, f32[16,16,256]{2,1,0:T(8,128)} %before_hbm.1, f32[16,16,256]{2,1,0:T(8,128)} %now_hbm.1, ...), custom_call_target="tpu_custom_call" | custom-call | tf_op jit(solution)/shard_map/pallas_call | solution.py:619
  23.1 1.0 %shard_map.130 = (f32[16,16,256]{2,1,0:T(8,128)}, f32[16,16,256]{2,1,0:T(8,128)}, f32[16,16,256]{2,1,0:T(8,128)}, f32[16,16,256]{2,1,0:T(8,128)}) custom-call(f32[8,128]{1,0:T(8,128)S(1)} %get-tuple-element.9.sums, f32[16,16,256]{2,1,0:T(8,128)S(1)} %get-tuple-element.10.v_next, f32[16,16,256]{2,1,0:T(8,128)S(1)} %get-tuple-element.11.v_after, ...), custom_call_target="tpu_custom_call" | custom-call | tf_op jit(solution)/shard_map/pallas_call | solution.py:682

commit v4 on v3

--- a/solution.py
+++ b/solution.py
@@ -91,7 +91,9 @@
     h1,
     h2,
     w1,
+    w1_rim,
     w2,
+    w2_short,
     w3,
     part,
     red,
@@ -372,31 +374,40 @@
             [rows_first(y - 2), rows_first(y - 1)], axis=0
         ).astype(BF16)
 
-    k2 = 8 * (blk + 2)
-    same_c = (iota((64, 3 * k2), 0) >> 3) == (iota((64, 3 * k2), 1) & 7)
-    a_in = third(iota((27, 3 * k2), 1), k2)
-    col = iota((8, 3 * k2), 1)
-    y_in = (col - k2 * third(col, k2)) >> 3
-    table = []
-    for t in range(9):
-        full = jnp.dot(
-            raw2[...], one_hot(iota((27, 3 * k2), 0) == 9 * a_in + t), preferred_element_type=F32
-        )
-        full = jnp.where(same_c, full, 0.0)
-        total = full[0:8]
-        for c in range(1, 8):
-            total = total + full[8 * c : 8 * c + 8]
-        table.append(total)
-
-    def rows_mid(i):
-        e, y = i // blk, i % blk
-        total = jnp.zeros((8, 3 * k2), F32)
-        for b in range(3):
-            total = jnp.where(y_in - y == b, table[3 * b + e], total)
-        return total
-
-    for i in range(0, 3 * blk, 2):
-        w2[8 * i : 8 * i + 16, :] = jnp.concatenate([rows_mid(i), rows_mid(i + 1)], axis=0).astype(BF16)
+    w1_rim[0:32] = w1[0:32]
+    w1_rim[32:64] = w1[m1 - 32 : m1]
+
+    def fill_mid(out, size):
+        wide = 8 * (size + 2)
+        same_c = (iota((64, 3 * wide), 0) >> 3) == (iota((64, 3 * wide), 1) & 7)
+        a_in = third(iota((27, 3 * wide), 1), wide)
+        col = iota((8, 3 * wide), 1)
+        y_in = (col - wide * third(col, wide)) >> 3
+        table = []
+        for t in range(9):
+            full = jnp.dot(
+                raw2[...], one_hot(iota((27, 3 * wide), 0) == 9 * a_in + t), preferred_element_type=F32
+            )
+            full = jnp.where(same_c, full, 0.0)
+            total = full[0:8]
+            for c in range(1, 8):
+                total = total + full[8 * c : 8 * c + 8]
+            table.append(total)
+
+        def rows_mid(i):
+            e, y = i // size, i % size
+            total = jnp.zeros((8, 3 * wide), F32)
+            for b in range(3):
+                total = jnp.where(y_in - y == b, table[3 * b + e], total)
+            return total
+
+        for i in range(0, 3 * size, 2):
+            out[8 * i : 8 * i + 16, :] = jnp.concatenate(
+                [rows_mid(i), rows_mid(i + 1)], axis=0
+            ).astype(BF16)
+
+    fill_mid(w2, blk)
+    fill_mid(w2_short, 4)
 
     same_c = iota((8, 3 * m2), 0) == (iota((8, 3 * m2), 1) & 7)
     a_in = third(iota((27, 3 * m2), 1), m2)
@@ -427,6 +438,10 @@
         from_own_x[i] = total
     for x in range(nx):
         from_own_y[x] = across(edge(ext_a[x + 4, own]))
+    ones = jnp.where(iota((8, depth), 0) < 3, 1.0, 0.0)
+    vacant = jnp.concatenate([jnp.zeros((24, depth), F32), ones], axis=0).astype(BF16)
+    for x in range(nx):
+        grad[x + 3, 3 * ny : 3 * ny + 32, :] = vacant
     for load in loads[8:]:
         load.wait()
 
@@ -470,7 +485,7 @@
         out_after[x] = value
         gradient = prior[x] + src[0, x] * center + src[1, x] * value
         out_grad[x] = gradient
-        store_own(x + 3, gradient)
+        grad[x + 3, ny : 2 * ny, :] = gradient.astype(BF16)
         return carry
 
     lax.fori_loop(0, nx, step_two, 0, unroll=WAVE_UNROLL)
@@ -478,56 +493,89 @@
         pack_g[0, t], pack_g[1, t] = pack_four([edge(out_grad[4 * t + j]) for j in range(4)])
     for c in copies_g:
         c.start()
-    for c in copies_g:
-        c.arrive()
-    ones = jnp.where(iota((8, depth), 0) < 3, 1.0, 0.0)
-    for t in range(groups + 2):
+    for x in range(nx):
+        for e in (0, 2):
+            grad[x + 3, ny * e : ny * e + ny, :] = shift_z(out_grad[x], e - 1).astype(BF16)
+
+    big = 3.0e38
+    x_low = jnp.where(gx == 0, 0.0, big)
+    x_high = jnp.where(gx == n_gx - 1, 0.0, big)
+    y_low = jnp.where(gy == 0, 0.0, big)
+    y_high = jnp.where(gy == n_gy - 1, 0.0, big)
+
+    def limit(value, cap):
+        return value if cap is None else jnp.minimum(value, cap)
+
+    def conv_plane(weight, rhs, rows):
+        res = jnp.dot(weight[...], rhs, preferred_element_type=F32)
+        return (
+            res[rows : 2 * rows] + shift_z(res[:rows], -1) + shift_z(res[2 * rows :], 1)
+        )
+
+    def layer_one(p, weight):
+        return jnp.maximum(
+            jnp.dot(weight, grad[p : p + 3].reshape(3 * slots, depth), preferred_element_type=F32), 0.0
+        )
+
+    def store_rim(p, low, high):
+        h1[p, 0:16] = jnp.minimum(low[0:16], y_low).astype(BF16)
+        h1[p, 16:32] = low[16:32].astype(BF16)
+        h1[p, m1 - 32 : m1 - 16] = high[0:16].astype(BF16)
+        h1[p, m1 - 16 : m1] = jnp.minimum(high[16:32], y_high).astype(BF16)
+
+    def layer_two(p, y, size, weight, cap):
+        rhs = h1[p : p + 3, 8 * y : 8 * y + 8 * size + 16, :].reshape(24 * size + 48, depth)
+        full = jnp.concatenate([jnp.broadcast_to(b2, (8, depth))] * size, axis=0)
+        res = limit(jnp.maximum(conv_plane(weight, rhs, 8 * size) + full, 0.0), cap)
+        if y == 0:
+            res = jnp.concatenate([jnp.minimum(res[0:8], y_low), res[8:]], axis=0)
+        if y + size == r2:
+            res = jnp.concatenate([res[: 8 * size - 8], jnp.minimum(res[8 * size - 8 :], y_high)], axis=0)
+        h2[p, 8 * y : 8 * y + 8 * size] = res.astype(BF16)
+
+    def fill_sides(t):
         for j, side in enumerate(unpack_four(recv_g[0, t], recv_g[1, t])):
             plane = 4 * t + j - 1
             if 0 <= plane < nx + 6:
                 grad[plane, 3 * ny : 3 * ny + 32, :] = jnp.concatenate(
                     [shift_z(side, -1), side, shift_z(side, 1), ones], axis=0
                 ).astype(BF16)
+
+    core_one = range(3, nx + 1)
+    core_two = range(3, nx - 1)
+    for p in core_one:
+        h1[p, 32 : m1 - 32] = layer_one(p, w1[32 : m1 - 32]).astype(BF16)
+    for p in core_two:
+        layer_two(p, 4, 6, w2, None)
+        layer_two(p, 10, 4, w2_short, None)
+    for c in copies_g[4:6]:
+        c.arrive()
+    for t in range(1, groups + 1):
+        fill_sides(t)
+    for p in core_one:
+        res = layer_one(p, w1_rim[...])
+        store_rim(p, res[0:32], res[32:64])
+    for p in core_two:
+        layer_two(p, 0, 4, w2_short, None)
+        layer_two(p, 14, 4, w2_short, None)
+    for c in copies_g[:4] + copies_g[6:]:
+        c.arrive()
+    for t in (0, groups + 1):
+        fill_sides(t)
     for i in range(3):
         store_own(i, recv_gx[0, i].astype(F32))
         store_own(nx + 3 + i, recv_gx[1, i].astype(F32))
-
-    big = 3.0e38
-    x_low = jnp.where(gx == 0, 0.0, big)
-    x_high = jnp.where(gx == n_gx - 1, 0.0, big)
-    y_low = jnp.where(gy == 0, 0.0, big)
-    y_high = jnp.where(gy == n_gy - 1, 0.0, big)
-
-    def conv_plane(weight, rhs, rows):
-        res = jnp.dot(weight[...], rhs, preferred_element_type=F32)
-        return (
-            res[rows : 2 * rows] + shift_z(res[:rows], -1) + shift_z(res[2 * rows :], 1)
-        )
-
-    def limit(value, cap):
-        return value if cap is None else jnp.minimum(value, cap)
-
     for p in range(nx + 4):
-        res = jnp.maximum(
-            jnp.dot(w1[...], grad[p : p + 3].reshape(3 * slots, depth), preferred_element_type=F32), 0.0
-        )
-        cap = x_low if p < 2 else x_high if p >= nx + 2 else None
-        res = limit(res, cap)
-        h1[p, 0:16] = jnp.minimum(res[0:16], y_low).astype(BF16)
-        h1[p, 16 : m1 - 16] = res[16 : m1 - 16].astype(BF16)
-        h1[p, m1 - 16 : m1] = jnp.minimum(res[m1 - 16 : m1], y_high).astype(BF16)
-
-    full2 = jnp.concatenate([jnp.broadcast_to(b2, (8, depth))] * blk, axis=0)
+        if p not in core_one:
+            cap = x_low if p < 2 else x_high if p >= nx + 2 else None
+            res = limit(layer_one(p, w1[...]), cap)
+            store_rim(p, res[0:32], res[m1 - 32 : m1])
+            h1[p, 32 : m1 - 32] = res[32 : m1 - 32].astype(BF16)
     for p in range(nx + 2):
-        cap = x_low if p < 1 else x_high if p >= nx + 1 else None
-        for y in range(0, r2, blk):
-            rhs = h1[p : p + 3, 8 * y : 8 * y + k2, :].reshape(3 * k2, depth)
-            res = limit(jnp.maximum(conv_plane(w2, rhs, 8 * blk) + full2, 0.0), cap)
-            if y == 0:
-                res = jnp.concatenate([jnp.minimum(res[0:8], y_low), res[8:]], axis=0)
-            if y + blk == r2:
-                res = jnp.concatenate([res[: 8 * blk - 8], jnp.minimum(res[8 * blk - 8 :], y_high)], axis=0)
-            h2[p, 8 * y : 8 * y + 8 * blk] = res.astype(BF16)
+        if p not in core_two:
+            cap = x_low if p < 1 else x_high if p >= nx + 1 else None
+            for y in range(0, r2, blk):
+                layer_two(p, y, blk, w2, cap)
 
     zero = jnp.zeros((ny, depth), F32)
 
@@ -650,7 +698,9 @@
             pltpu.VMEM((nx + 4, r1 * ch, depth), BF16),
             pltpu.VMEM((nx + 2, r2 * ch, depth), BF16),
             pltpu.VMEM((r1 * ch, 3 * slots), BF16),
+            pltpu.VMEM((64, 3 * slots), BF16),
             pltpu.VMEM((3 * blk * ch, 3 * (blk + 2) * ch), BF16),
+            pltpu.VMEM((12 * ch, 18 * ch), BF16),
             pltpu.VMEM((3 * ny, 3 * r2 * ch), BF16),
             pltpu.VMEM((1, 128), F32),
             pltpu.VMEM((count - 1, 1, 128), F32),

time: 24.2 us -> 23.2 us (0.959)
  Pallas kernels: 23.4 us -> 22.4 us
    pallas_call x1, Pallas kernels: 22.4 us -> 21.4 us  [shards(): pl.pallas_call(functools.partial(kernel, n_gx, n_gy), out_shape=(held,) *...]
where the time goes in v4:
time: 23.2 us; the launch traced here: 23.1 us
  Pallas kernels  22.4 us (97%)
  between operations  0.64 us (3%)
    pallas_call x1, Pallas kernels, shards(): pl.pallas_call(functools.partial(kernel, n_gx, n_gy), out_shape=(held,) *...  21.4 us
    pallas_call x1, Pallas kernels, shards(): pl.pallas_call(functools.partial(hand_on, 8.0 * float(nx * n_gx * ny * n_...  1.02 us

profile of v4, /device:TPU:0, one launch (start us, length us, event | category | flops | bytes accessed | tf_op | source)
XLA Modules:
  0.0 23.1 jit_solution(9026964231618909761)
XLA Ops:
  0.6 21.4 %shard_map.129 = (f32[16,16,256]{2,1,0:T(8,128)S(1)}, f32[16,16,256]{2,1,0:T(8,128)S(1)}, f32[16,16,256]{2,1,0:T(8,128)S(1)}, f32[16,16,256]{2,1,0:T(8,128)S(1)}, f32[8,128]{1,0:T(8,128)S(1)}) custom-call(f32[16,16,256]{2,1,0:T(8,128)} %speed_hbm.1, f32[16,16,256]{2,1,0:T(8,128)} %before_hbm.1, f32[16,16,256]{2,1,0:T(8,128)} %now_hbm.1, ...), custom_call_target="tpu_custom_call" | custom-call | tf_op jit(solution)/shard_map/pallas_call | solution.py:667
  22.0 1.0 %shard_map.130 = (f32[16,16,256]{2,1,0:T(8,128)}, f32[16,16,256]{2,1,0:T(8,128)}, f32[16,16,256]{2,1,0:T(8,128)}, f32[16,16,256]{2,1,0:T(8,128)}) custom-call(f32[8,128]{1,0:T(8,128)S(1)} %get-tuple-element.9.sums, f32[16,16,256]{2,1,0:T(8,128)S(1)} %get-tuple-element.10.v_next, f32[16,16,256]{2,1,0:T(8,128)S(1)} %get-tuple-element.11.v_after, ...), custom_call_target="tpu_custom_call" | custom-call | tf_op jit(solution)/shard_map/pallas_call | solution.py:732

commit v5 on v4

--- a/solution.py
+++ b/solution.py
@@ -33,16 +33,6 @@
 
 def third(index, size):
     return jnp.where(index >= size, 1, 0) + jnp.where(index >= 2 * size, 1, 0)
-
-
-def laplace_xy(ext, x, ny):
-    total = None
-    for k in range(1, 5):
-        cycle = ext[x + 4 + k, 8 : 8 + ny, :] + ext[x + 4 - k, 8 : 8 + ny, :]
-        cycle = cycle + ext[x + 4, 8 + k : 8 + k + ny, :]
-        cycle = cycle + ext[x + 4, 8 - k : 8 - k + ny, :]
-        total = COEFS[k] * cycle if total is None else total + COEFS[k] * cycle
-    return total
 
 
 def kernel(
@@ -73,8 +63,9 @@
     bias1,
     bias2,
     load_sem,
-    ext_a,
-    ext_b,
+    now,
+    star,
+    wave,
     pack_x,
     pack_y,
     recv_x,
@@ -105,12 +96,11 @@
     nx, ny, depth = now_hbm.shape
     gx, gy = lax.axis_index("gx"), lax.axis_index("gy")
     barrier = pltpu.get_barrier_semaphore()
-    brick = pl.ds(8, ny)
     loads = [
         pltpu.make_async_copy(source, target, load_sem.at[i])
         for i, (source, target) in enumerate(
             (
-                (now_hbm, ext_a.at[pl.ds(4, nx), brick, :]),
+                (now_hbm, now),
                 (before_hbm, before),
                 (speed_hbm, speed),
                 (first_hbm, raw1),
@@ -123,7 +113,7 @@
             )
         )
     ]
-    for load in loads:
+    for load in loads[:3]:
         load.start()
 
     def there(dx, dy):
@@ -152,6 +142,9 @@
         @pl.when(there(dx, dy))
         def _(dx=dx, dy=dy):
             greet(gx + dx, gy + dy)
+
+    for load in loads[3:]:
+        load.start()
 
     def far(pos, j):
         return (j - pos > FAR) | (pos - j > FAR)
@@ -275,36 +268,45 @@
     stencil[0] = taps.astype(BF16)
     stencil[1] = (taps - taps.astype(BF16).astype(F32)).astype(BF16)
 
-    def along_z(field):
-        v = field.reshape(nx * ny, depth)
+    cells = nx * ny
+    bits = ny.bit_length() - 1
+
+    def split(v):
         high = v.astype(BF16)
-        low = (v - high.astype(F32)).astype(BF16)
-
-        def times(x, i):
-            return jnp.dot(x, stencil[i], preferred_element_type=F32)
-
-        total = times(high, 0) + times(high, 1) + times(low, 0)
+        return high, (v - high.astype(F32)).astype(BF16)
+
+    def fill_star(start, width, place):
+        row, col = iota((cells, width), 0), iota((cells, width), 1)
+        x_in, y_in = place(col)
+        dx, dy = x_in - (row >> bits), y_in - (row & (ny - 1))
+        far = jnp.where(dx == 0, jnp.abs(dy), jnp.where(dy == 0, jnp.abs(dx), 0))
+        value = jnp.zeros((cells, width), F32)
+        for k in range(1, 5):
+            value = jnp.where(far == k, COEFS[k], value)
+        at = slice(start, start + width)
+        star[0, :, at], star[1, :, at] = split(value)
+
+    def laplace(high, low, width):
+        def times(x, y):
+            return jnp.dot(x, y, preferred_element_type=F32)
+
+        total = times(high[0:cells], stencil[0]) + times(high[0:cells], stencil[1])
+        total = total + times(low[0:cells], stencil[0])
+        total = total + times(star[0, :, 0:width], high[0:width]) + times(star[1, :, 0:width], high[0:width])
+        total = total + times(star[0, :, 0:width], low[0:width])
         lap_z[...] = total.reshape(nx, ny, depth)
 
-    blank = jnp.zeros((ny + 16, depth), F32)
-    for i in range(4):
-        ext_a[i] = blank
-        ext_a[nx + 4 + i] = blank
-    for x in range(nx):
-        ext_a[x + 4, 0:8] = blank[0:8]
-        ext_a[x + 4, ny + 8 : ny + 16] = blank[0:8]
+    fill_star(0, cells, lambda col: (col >> bits, col & (ny - 1)))
     for load in loads[:3]:
         load.wait()
 
-    along_z(ext_a[4 : 4 + nx, 8 : 8 + ny, :])
+    laplace(*split(now[...].reshape(cells, depth)), cells)
     for t in range(groups):
         edges = [[], [], []]
         for x in range(4 * t, 4 * t + 4):
-            center = ext_a[x + 4, 8 : 8 + ny, :]
+            center = now[x]
             factor = speed[x]
-            partial = (
-                2.0 * center - before[x] + factor * (lap_z[x] + laplace_xy(ext_a, x, ny))
-            )
+            partial = 2.0 * center - before[x] + factor * lap_z[x]
             out_next[x] = partial
             for i, v in enumerate((center, partial, factor)):
                 edges[i].append(edge(v))
@@ -425,7 +427,6 @@
             total = jnp.where(gap == b, jnp.broadcast_to(line, total.shape), total)
         w3[ny * e : ny * e + ny, :] = total.astype(BF16)
 
-    own = slice(8, 8 + ny)
     outside = [x for x in range(-4, nx + 4) if x < 0 or x >= nx]
 
     def reach(x, inside):
@@ -434,10 +435,20 @@
     for i, x in enumerate(outside):
         total = jnp.zeros((ny, depth), F32)
         for k, at in reach(x, lambda v: 0 <= v < nx):
-            total = total + COEFS[k] * ext_a[at + 4, own]
+            total = total + COEFS[k] * now[at]
         from_own_x[i] = total
     for x in range(nx):
-        from_own_y[x] = across(edge(ext_a[x + 4, own]))
+        from_own_y[x] = across(edge(now[x]))
+    fill_star(
+        cells,
+        8 * ny,
+        lambda col: ((col >> bits) + jnp.where((col >> bits) < 4, -4, nx - 4), col & (ny - 1)),
+    )
+    fill_star(
+        cells + 8 * ny,
+        8 * nx,
+        lambda col: (col >> 3, (col & 7) + jnp.where((col & 7) < 4, ny, -8)),
+    )
     ones = jnp.where(iota((8, depth), 0) < 3, 1.0, 0.0)
     vacant = jnp.concatenate([jnp.zeros((24, depth), F32), ones], axis=0).astype(BF16)
     for x in range(nx):
@@ -447,6 +458,10 @@
 
     for c in copies_w:
         c.arrive()
+    def keep(start, value):
+        at = slice(start, start + value.shape[0])
+        wave[0, at], wave[1, at] = split(value)
+
     corner = {}
     for i, first in enumerate((-4, nx)):
         for j, v in enumerate(unpack_four(recv_c[i, 0], recv_c[i, 1])):
@@ -454,7 +469,7 @@
     halo_x = {x: recv_x.at[i // 4, i % 4] for i, x in enumerate(outside)}
     for i, x in enumerate(outside):
         felt = from_own_x[i] + spread(across(corner[x]))
-        ext_b[x + 4, own] = halo_x[x][1].astype(F32) + halo_x[x][2].astype(F32) * felt
+        keep(cells + ny * i, halo_x[x][1].astype(F32) + halo_x[x][2].astype(F32) * felt)
     for t in range(groups):
         sides = [unpack_four(recv_y[0, t, i], recv_y[1, t, i]) for i in range(3)]
         for j in range(4):
@@ -463,25 +478,26 @@
             for k, at in reach(x, lambda v: v in corner):
                 felt = felt + COEFS[k] * corner[at]
             side = sides[1][j] + sides[2][j] * felt
-            ext_b[x + 4, 0:8] = side
-            ext_b[x + 4, ny + 8 : ny + 16] = side
+            if x % 2:
+                keep(cells + 8 * ny + 8 * (x - 1), jnp.concatenate([before_side, side], axis=0))
+            before_side = side
             felt = spread(across(sides[0][j]))
             for k, at in reach(x, lambda v: v in corner):
                 felt = felt + COEFS[k] * halo_x[at][0].astype(F32)
             value = out_next[x] + speed[x] * felt
             out_next[x] = value
-            ext_b[x + 4, own] = value
+            keep(ny * x, value)
 
     def store_own(plane, value):
         for e in range(3):
             rows = value if e == 1 else shift_z(value, e - 1)
             grad[plane, ny * e : ny * e + ny, :] = rows.astype(BF16)
 
-    along_z(out_next[...])
+    laplace(wave.at[0], wave.at[1], cells + 8 * ny + 8 * nx)
 
     def step_two(x, carry):
         center = out_next[x]
-        value = 2.0 * center - ext_a[x + 4, own] + speed[x] * (lap_z[x] + laplace_xy(ext_b, x, ny))
+        value = 2.0 * center - now[x] + speed[x] * lap_z[x]
         out_after[x] = value
         gradient = prior[x] + src[0, x] * center + src[1, x] * value
         out_grad[x] = gradient
@@ -558,6 +574,20 @@
     for p in core_two:
         layer_two(p, 0, 4, w2_short, None)
         layer_two(p, 14, 4, w2_short, None)
+    zero = jnp.zeros((ny, depth), F32)
+
+    def layer_three(p, carry):
+        gg, gd, dd = carry
+        rhs = h2[p : p + 3].reshape(3 * m2, depth)
+        g = out_grad[p]
+        d = conv_plane(w3, rhs, ny) + g
+        out_dir[p] = d
+        return gg + g * g, gd + g * d, dd + d * d
+
+    sums = (zero, zero, zero)
+    core_three = range(3, nx - 3)
+    for p in core_three:
+        sums = layer_three(p, sums)
     for c in copies_g[:4] + copies_g[6:]:
         c.arrive()
     for t in (0, groups + 1):
@@ -577,17 +607,9 @@
             for y in range(0, r2, blk):
                 layer_two(p, y, blk, w2, cap)
 
-    zero = jnp.zeros((ny, depth), F32)
-
-    def layer_three(p, carry):
-        gg, gd, dd = carry
-        rhs = h2[pl.ds(p, 3)].reshape(3 * m2, depth)
-        g = out_grad[p]
-        d = conv_plane(w3, rhs, ny) + g
-        out_dir[p] = d
-        return gg + g * g, gd + g * d, dd + d * d
-
-    sums = lax.fori_loop(0, nx, layer_three, (zero, zero, zero), unroll=UNROLL)
+    for p in range(nx):
+        if p not in core_three:
+            sums = layer_three(p, sums)
     row, lane = iota((8, 128), 0), iota((8, 128), 1)
     tile = jnp.zeros((8, 128), F32)
     for i, s in enumerate(sums):
@@ -603,34 +625,31 @@
         pltpu.make_async_remote_copy(
             src_ref=part,
             dst_ref=red.at[i - 1],
-            send_sem=red_send.at[i - 1],
-            recv_sem=red_recv.at[i - 1],
+            send_sem=red_send,
+            recv_sem=red_recv,
             device_id=peer(i),
             device_id_type=MESH,
         ).start()
-    waits = [
-        pltpu.make_async_remote_copy(
-            src_ref=part,
-            dst_ref=red.at[i - 1],
-            send_sem=red_send.at[i - 1],
-            recv_sem=red_recv.at[i - 1],
-            device_id=peer(i),
-            device_id_type=MESH,
-        )
-        for i in range(1, count)
-    ]
-    for c in waits:
-        c.wait_recv()
-    total = mine
-    for i in range(count - 1):
-        total = total + red[i]
-    spread = jnp.where(row == lane, jnp.broadcast_to(total, (8, 128)), 0.0)
-    out_sums[...] = jnp.broadcast_to(jnp.sum(spread, axis=1, keepdims=True), (8, 128))
     for group in (copies_w, copies_g):
         for c in group:
             c.sent()
-    for c in waits:
-        c.wait_send()
+    every = pltpu.make_async_remote_copy(
+        src_ref=red,
+        dst_ref=red,
+        send_sem=red_send,
+        recv_sem=red_recv,
+        device_id=peer(1),
+        device_id_type=MESH,
+    )
+    every.wait_recv()
+    terms = [mine] + [red[i] for i in range(count - 1)]
+    while len(terms) > 1:
+        pairs = [terms[i] + terms[i + 1] for i in range(0, len(terms) - 1, 2)]
+        terms = pairs + terms[2 * len(pairs) :]
+    total = terms[0]
+    spread = jnp.where(row == lane, jnp.broadcast_to(total, (8, 128)), 0.0)
+    out_sums[...] = jnp.broadcast_to(jnp.sum(spread, axis=1, keepdims=True), (8, 128))
+    every.wait_send()
 
 
 def hand_on(damping, sums, v_next, v_after, v_grad, v_dir, o_next, o_after, o_grad, o_step, scaled, sem):
@@ -680,8 +699,9 @@
             pltpu.VMEM((1, ch), F32),
             pltpu.VMEM((1, ch), F32),
             pltpu.SemaphoreType.DMA((10,)),
-            pltpu.VMEM((nx + 8, ny + 16, depth), F32),
-            pltpu.VMEM((nx + 8, ny + 16, depth), F32),
+            pltpu.VMEM(now.shape, F32),
+            pltpu.VMEM((2, nx * ny, nx * ny + 8 * ny + 8 * nx), BF16),
+            pltpu.VMEM((2, nx * ny + 8 * ny + 8 * nx, depth), BF16),
             pltpu.VMEM((2, 4, 3, ny, depth), BF16),
             pltpu.VMEM((2, groups, 3, 16, depth), BF16),
             pltpu.VMEM((2, 4, 3, ny, depth), BF16),
@@ -706,8 +726,8 @@
             pltpu.VMEM((count - 1, 1, 128), F32),
             pltpu.SemaphoreType.DMA((16,)),
             pltpu.SemaphoreType.DMA((16,)),
-            pltpu.SemaphoreType.DMA((count - 1,)),
-            pltpu.SemaphoreType.DMA((count - 1,)),
+            pltpu.SemaphoreType.DMA,
+            pltpu.SemaphoreType.DMA,
         ],
         compiler_params=pltpu.CompilerParams(
             collective_id=0, has_side_effects=True, vmem_limit_bytes=40 * 1024 * 1024

time: 23.2 us -> 22.5 us (0.970)
  Pallas kernels: 22.4 us -> 21.7 us
    pallas_call x1, Pallas kernels: 21.4 us -> 20.7 us  [shards(): pl.pallas_call(functools.partial(kernel, n_gx, n_gy), out_shape=(held,) *...]
where the time goes in v5:
time: 22.5 us; the launch traced here: 22.3 us
  Pallas kernels  21.7 us (96%)
  between operations  0.64 us (3%)
    pallas_call x1, Pallas kernels, shards(): pl.pallas_call(functools.partial(kernel, n_gx, n_gy), out_shape=(held,) *...  20.7 us
    pallas_call x1, Pallas kernels, shards(): pl.pallas_call(functools.partial(hand_on, 8.0 * float(nx * n_gx * ny * n_...  1.02 us

profile of v5, /device:TPU:0, one launch (start us, length us, event | category | flops | bytes accessed | tf_op | source)
XLA Modules:
  0.0 22.3 jit_solution(7141384600819887207)
XLA Ops:
  0.6 20.7 %shard_map.129 = (f32[16,16,256]{2,1,0:T(8,128)S(1)}, f32[16,16,256]{2,1,0:T(8,128)S(1)}, f32[16,16,256]{2,1,0:T(8,128)S(1)}, f32[16,16,256]{2,1,0:T(8,128)S(1)}, f32[8,128]{1,0:T(8,128)S(1)}) custom-call(f32[16,16,256]{2,1,0:T(8,128)} %speed_hbm.1, f32[16,16,256]{2,1,0:T(8,128)} %before_hbm.1, f32[16,16,256]{2,1,0:T(8,128)} %now_hbm.1, ...), custom_call_target="tpu_custom_call" | custom-call | tf_op jit(solution)/shard_map/pallas_call | solution.py:686
  21.3 1.0 %shard_map.130 = (f32[16,16,256]{2,1,0:T(8,128)}, f32[16,16,256]{2,1,0:T(8,128)}, f32[16,16,256]{2,1,0:T(8,128)}, f32[16,16,256]{2,1,0:T(8,128)}) custom-call(f32[8,128]{1,0:T(8,128)S(1)} %get-tuple-element.9.sums, f32[16,16,256]{2,1,0:T(8,128)S(1)} %get-tuple-element.10.v_next, f32[16,16,256]{2,1,0:T(8,128)S(1)} %get-tuple-element.11.v_after, ...), custom_call_target="tpu_custom_call" | custom-call | tf_op jit(solution)/shard_map/pallas_call | solution.py:752

commit v6 on v5

--- a/solution.py
+++ b/solution.py
@@ -495,19 +495,25 @@
 
     laplace(wave.at[0], wave.at[1], cells + 8 * ny + 8 * nx)
 
-    def step_two(x, carry):
-        center = out_next[x]
-        value = 2.0 * center - now[x] + speed[x] * lap_z[x]
-        out_after[x] = value
-        gradient = prior[x] + src[0, x] * center + src[1, x] * value
-        out_grad[x] = gradient
-        grad[x + 3, ny : 2 * ny, :] = gradient.astype(BF16)
-        return carry
-
-    lax.fori_loop(0, nx, step_two, 0, unroll=WAVE_UNROLL)
-    for t in range(groups):
-        pack_g[0, t], pack_g[1, t] = pack_four([edge(out_grad[4 * t + j]) for j in range(4)])
-    for c in copies_g:
+    def step_two(t):
+        edges = []
+        for x in range(4 * t, 4 * t + 4):
+            center = out_next[x]
+            value = 2.0 * center - now[x] + speed[x] * lap_z[x]
+            out_after[x] = value
+            gradient = prior[x] + src[0, x] * center + src[1, x] * value
+            out_grad[x] = gradient
+            grad[x + 3, ny : 2 * ny, :] = gradient.astype(BF16)
+            edges.append(edge(gradient))
+        pack_g[0, t], pack_g[1, t] = pack_four(edges)
+
+    step_two(0)
+    step_two(groups - 1)
+    for c in copies_g[:4] + copies_g[6:]:
+        c.start()
+    for t in range(1, groups - 1):
+        step_two(t)
+    for c in copies_g[4:6]:
         c.start()
     for x in range(nx):
         for e in (0, 2):

time: 22.5 us -> 22.4 us (level)
  no operation moved by 1% of the time
where the time goes in v6:
time: 22.4 us; the launch traced here: 22.2 us
  Pallas kernels  21.6 us (96%)
  between operations  0.64 us (3%)
    pallas_call x1, Pallas kernels, shards(): pl.pallas_call(functools.partial(kernel, n_gx, n_gy), out_shape=(held,) *...  20.6 us
    pallas_call x1, Pallas kernels, shards(): pl.pallas_call(functools.partial(hand_on, 8.0 * float(nx * n_gx * ny * n_...  1.02 us

profile of v6, /device:TPU:0, one launch (start us, length us, event | category | flops | bytes accessed | tf_op | source)
XLA Modules:
  0.0 22.2 jit_solution(11531270749754577873)
XLA Ops:
  0.6 20.6 %shard_map.129 = (f32[16,16,256]{2,1,0:T(8,128)S(1)}, f32[16,16,256]{2,1,0:T(8,128)S(1)}, f32[16,16,256]{2,1,0:T(8,128)S(1)}, f32[16,16,256]{2,1,0:T(8,128)S(1)}, f32[8,128]{1,0:T(8,128)S(1)}) custom-call(f32[16,16,256]{2,1,0:T(8,128)} %speed_hbm.1, f32[16,16,256]{2,1,0:T(8,128)} %before_hbm.1, f32[16,16,256]{2,1,0:T(8,128)} %now_hbm.1, ...), custom_call_target="tpu_custom_call" | custom-call | tf_op jit(solution)/shard_map/pallas_call | solution.py:692
  21.2 1.0 %shard_map.130 = (f32[16,16,256]{2,1,0:T(8,128)}, f32[16,16,256]{2,1,0:T(8,128)}, f32[16,16,256]{2,1,0:T(8,128)}, f32[16,16,256]{2,1,0:T(8,128)}) custom-call(f32[8,128]{1,0:T(8,128)S(1)} %get-tuple-element.9.sums, f32[16,16,256]{2,1,0:T(8,128)S(1)} %get-tuple-element.10.v_next, f32[16,16,256]{2,1,0:T(8,128)S(1)} %get-tuple-element.11.v_after, ...), custom_call_target="tpu_custom_call" | custom-call | tf_op jit(solution)/shard_map/pallas_call | solution.py:758

commit v7 on v6

--- a/solution.py
+++ b/solution.py
@@ -601,21 +601,31 @@
     for i in range(3):
         store_own(i, recv_gx[0, i].astype(F32))
         store_own(nx + 3 + i, recv_gx[1, i].astype(F32))
-    for p in range(nx + 4):
-        if p not in core_one:
-            cap = x_low if p < 2 else x_high if p >= nx + 2 else None
-            res = limit(layer_one(p, w1[...]), cap)
-            store_rim(p, res[0:32], res[m1 - 32 : m1])
-            h1[p, 32 : m1 - 32] = res[32 : m1 - 32].astype(BF16)
-    for p in range(nx + 2):
-        if p not in core_two:
-            cap = x_low if p < 1 else x_high if p >= nx + 1 else None
-            for y in range(0, r2, blk):
-                layer_two(p, y, blk, w2, cap)
-
-    for p in range(nx):
-        if p not in core_three:
-            sums = layer_three(p, sums)
+    def rim_one(p):
+        cap = x_low if p < 2 else x_high if p >= nx + 2 else None
+        res = limit(layer_one(p, w1[...]), cap)
+        store_rim(p, res[0:32], res[m1 - 32 : m1])
+        h1[p, 32 : m1 - 32] = res[32 : m1 - 32].astype(BF16)
+
+    def rim_two(p):
+        cap = x_low if p < 1 else x_high if p >= nx + 1 else None
+        for y in range(0, r2, blk):
+            layer_two(p, y, blk, w2, cap)
+
+    last = nx + 3
+    for p in (2, last - 2):
+        rim_one(p)
+    for p, q in ((2, 1), (nx - 1, last - 1)):
+        rim_two(p)
+        rim_one(q)
+    for p, q in ((1, 0), (nx, last)):
+        rim_two(p)
+        rim_one(q)
+    for p, q in ((2, 0), (nx - 3, nx + 1)):
+        sums = layer_three(p, sums)
+        rim_two(q)
+    for p in (1, nx - 2, 0, nx - 1):
+        sums = layer_three(p, sums)
     row, lane = iota((8, 128), 0), iota((8, 128), 1)
     tile = jnp.zeros((8, 128), F32)
     for i, s in enumerate(sums):

time: 22.4 us -> 22.5 us (level)
  no operation moved by 1% of the time
where the time goes in v7:
time: 22.5 us; the launch traced here: 22.3 us
  Pallas kernels  21.7 us (96%)
  between operations  0.64 us (3%)
    pallas_call x1, Pallas kernels, shards(): pl.pallas_call(functools.partial(kernel, n_gx, n_gy), out_shape=(held,) *...  20.7 us
    pallas_call x1, Pallas kernels, shards(): pl.pallas_call(functools.partial(hand_on, 8.0 * float(nx * n_gx * ny * n_...  1.02 us

profile of v7, /device:TPU:0, one launch (start us, length us, event | category | flops | bytes accessed | tf_op | source)
XLA Modules:
  0.0 22.3 jit_solution(17467165732309717164)
XLA Ops:
  0.6 20.7 %shard_map.129 = (f32[16,16,256]{2,1,0:T(8,128)S(1)}, f32[16,16,256]{2,1,0:T(8,128)S(1)}, f32[16,16,256]{2,1,0:T(8,128)S(1)}, f32[16,16,256]{2,1,0:T(8,128)S(1)}, f32[8,128]{1,0:T(8,128)S(1)}) custom-call(f32[16,16,256]{2,1,0:T(8,128)} %speed_hbm.1, f32[16,16,256]{2,1,0:T(8,128)} %before_hbm.1, f32[16,16,256]{2,1,0:T(8,128)} %now_hbm.1, ...), custom_call_target="tpu_custom_call" | custom-call | tf_op jit(solution)/shard_map/pallas_call | solution.py:702
  21.3 1.0 %shard_map.130 = (f32[16,16,256]{2,1,0:T(8,128)}, f32[16,16,256]{2,1,0:T(8,128)}, f32[16,16,256]{2,1,0:T(8,128)}, f32[16,16,256]{2,1,0:T(8,128)}) custom-call(f32[8,128]{1,0:T(8,128)S(1)} %get-tuple-element.9.sums, f32[16,16,256]{2,1,0:T(8,128)S(1)} %get-tuple-element.10.v_next, f32[16,16,256]{2,1,0:T(8,128)S(1)} %get-tuple-element.11.v_after, ...), custom_call_target="tpu_custom_call" | custom-call | tf_op jit(solution)/shard_map/pallas_call | solution.py:768
